TPU v7x, 128 devices: a whole 4x4x4 slice. The times are simulated.
128 devices in a mesh: lon: 32 (over x, z, y_hi), grp: 4 (over y_lo, core).
Axes of the slice: x: 4, y: 4 (y_hi: 2, y_lo: 2; y = y_hi * 2 + y_lo), z: 4, core: 2. Of those that a mesh axis runs over, the one named last changes fastest.
Arguments:
- features: bfloat16 [64, 4096, 128], P('grp', 'lon'), may hold values from -6 to 6
- conv_one_w: bfloat16 [3, 3, 128, 128], replicated, may hold values from -0.1875 to 0.1875
- conv_one_b: float32 [128], replicated, may hold values from -3 to 3
- conv_two_w: bfloat16 [3, 3, 128, 128], replicated, may hold values from -0.1875 to 0.1875
- conv_two_b: float32 [128], replicated, may hold values from -3 to 3
- out_conv_w: bfloat16 [3, 3, 128, 3], replicated, may hold values from -0.1875 to 0.1875
- out_conv_b: float32 [3], replicated, may hold values from -3 to 3
- vgg_one_w: bfloat16 [64, 3, 3, 3], replicated, may hold values from -1.25 to 1.25
- vgg_one_b: float32 [64], replicated, may hold values from -3 to 3
- vgg_two_w: bfloat16 [64, 64, 3, 3], replicated, may hold values from -0.25 to 0.25
- vgg_two_b: float32 [64], replicated, may hold values from -3 to 3
- lin_weights: float32 [64], replicated, may hold values from 0.1 to 1
- row_lists: int32 [128, 3, 8], P(('lon', 'grp')), may hold values from 0 to 15, as said below
- tap_index: int32 [128, 4, 8192], P(('lon', 'grp')), may hold values from 0 to 3071, as said below
- tap_weight: float32 [128, 4, 8192], P(('lon', 'grp')), may hold values from 0 to 1, as said below
- target_tiles: bfloat16 [128, 3, 64, 128], P(('lon', 'grp')), may hold values from -3 to 3
Outputs:
- loss: float32 [], replicated
- grad_one: float32 [3, 3, 128, 128], replicated
- grad_two: float32 [3, 3, 128, 128], replicated
- grad_out: float32 [3, 3, 128, 3], replicated
Inputs may be any that keep to these rules, and one draw needn't show every extreme that they name: `row_lists`: each list is 8 consecutive rows of the sending slab, and the three slabs that serve one tile send the same rows. `tap_index`: the four taps of a pixel are the corners of one cell: slots j and j + 1 of one offset, columns x and x + 1 of the three slabs laid side by side from west to east. `tap_weight`: the four weights of a pixel are the bilinear weights of that cell: non-negative, summing to one.
All inputs are finite; a program needn't handle non-finite values.
Results may differ from a plain program's by a relative error of at most 0.0055.
Values may be sent and summed in bfloat16 or wider, within the bound.
A program may use at most 128 MiB of HBM per device.

v0:
```python
import jax
import jax.numpy as jnp
from jax import lax
from jax.sharding import PartitionSpec as P

offset_rgb = (-0.03, -0.088, -0.188)
spread_rgb = (0.458, 0.448, 0.45)
loss_scale = 64.0


def extended(cells, sides, width, closed):
    for axis, dim in sides:
        count = lax.axis_size(axis)
        ends = count if closed else count - 1
        head = lax.slice_in_dim(cells, 0, width, axis=dim)
        tail = lax.slice_in_dim(cells, cells.shape[dim] - width, cells.shape[dim], axis=dim)
        cells = jnp.concatenate(
            [
                lax.ppermute(tail, axis, [(i, (i + 1) % count) for i in range(ends)]),
                cells,
                lax.ppermute(head, axis, [((i + 1) % count, i) for i in range(ends)]),
            ],
            axis=dim,
        )
    return cells


def from_behind(array, axis, by):
    peers = lax.axis_size(axis)
    return lax.ppermute(array, axis, [(i, (i + by) % peers) for i in range(peers)])


def conv_valid(padded, weight):
    return lax.conv_general_dilated(
        padded[None],
        weight,
        (1, 1),
        "VALID",
        dimension_numbers=("NHWC", "HWIO", "NHWC"),
        preferred_element_type=jnp.float32,
    )[0]


def conv_same(picture, weight):
    return lax.conv_general_dilated(
        picture[None],
        weight,
        (1, 1),
        "SAME",
        dimension_numbers=("NCHW", "OIHW", "NCHW"),
        preferred_element_type=jnp.float32,
    )[0]


def flip_weight(weight):
    return jnp.transpose(weight[::-1, ::-1], (0, 1, 3, 2))


def weight_grad(padded, adjoint):
    height, breadth, out_channels = adjoint.shape
    in_channels = padded.shape[2]
    flat_adjoint = adjoint.reshape(height * breadth, out_channels)
    pieces = []
    for offset_y in range(3):
        for offset_x in range(3):
            window = padded[offset_y : offset_y + height, offset_x : offset_x + breadth].reshape(
                height * breadth, in_channels
            )
            pieces.append(
                lax.dot_general(
                    window,
                    flat_adjoint,
                    (((0,), (0,)), ((), ())),
                    preferred_element_type=jnp.float32,
                )
            )
    return jnp.stack(pieces).reshape(3, 3, in_channels, out_channels)


def silu_slope(hidden):
    hidden_f32 = hidden.astype(jnp.float32)
    sigmoid_val = jax.nn.sigmoid(hidden_f32)
    return sigmoid_val * (1.0 + hidden_f32 * (1.0 - sigmoid_val))


def silu_round(hidden):
    return jax.nn.silu(hidden.astype(jnp.float32)).astype(jnp.bfloat16)


def cycle_rims(grid_field):
    widened = extended(grid_field, (("lon", 1),), 1, True)
    return extended(widened, (("grp", 0),), 1, False)


def decoder_forward(
    features, conv_one_w, conv_one_b, conv_two_w, conv_two_b, out_conv_w, out_conv_b
):
    pad_zero = cycle_rims(silu_round(features))
    hidden_one = (conv_valid(pad_zero, conv_one_w) + conv_one_b).astype(jnp.bfloat16)
    pad_one = cycle_rims(silu_round(hidden_one))
    hidden_two = (
        features.astype(jnp.float32) + conv_valid(pad_one, conv_two_w) + conv_two_b
    ).astype(jnp.bfloat16)
    pad_two = cycle_rims(silu_round(hidden_two))
    colour = conv_valid(pad_two, out_conv_w) + out_conv_b
    return (colour, (pad_zero, hidden_one, pad_one, hidden_two, pad_two))


def decoder_backward(colour_adj, saved, conv_two_w, out_conv_w):
    pad_zero, hidden_one, pad_one, hidden_two, pad_two = saved
    adj_three = colour_adj.astype(jnp.bfloat16)
    grad_out = weight_grad(pad_two, adj_three)
    adj_two = (
        conv_valid(cycle_rims(adj_three), flip_weight(out_conv_w)) * silu_slope(hidden_two)
    ).astype(jnp.bfloat16)
    grad_two = weight_grad(pad_one, adj_two)
    adj_one = (
        conv_valid(cycle_rims(adj_two), flip_weight(conv_two_w)) * silu_slope(hidden_one)
    ).astype(jnp.bfloat16)
    grad_one = weight_grad(pad_zero, adj_one)
    return (grad_one, grad_two, grad_out)


def vgg_block(picture, vgg_one_w, vgg_one_b, vgg_two_w, vgg_two_b):
    offset = jnp.array(offset_rgb, jnp.float32)[:, None, None]
    spread = jnp.array(spread_rgb, jnp.float32)[:, None, None]
    scaled = ((picture.astype(jnp.float32) - offset) / spread).astype(jnp.bfloat16)
    first_layer = jax.nn.relu(conv_same(scaled, vgg_one_w) + vgg_one_b[:, None, None]).astype(
        jnp.bfloat16
    )
    return jax.nn.relu(conv_same(first_layer, vgg_two_w) + vgg_two_b[:, None, None])


def unit_norm(feature):
    return feature * lax.rsqrt(jnp.sum(feature * feature, axis=0, keepdims=True) + 1e-05)


def tile_loss(predicted, target, vgg_one_w, vgg_one_b, vgg_two_w, vgg_two_b, lin_weights):
    height, breadth = (target.shape[1], target.shape[2])
    pred_feat = vgg_block(
        predicted.reshape(3, height, breadth), vgg_one_w, vgg_one_b, vgg_two_w, vgg_two_b
    )
    true_feat = vgg_block(target, vgg_one_w, vgg_one_b, vgg_two_w, vgg_two_b)
    difference = unit_norm(pred_feat) - unit_norm(true_feat)
    return jnp.mean(jnp.sum(lin_weights[:, None, None] * difference * difference, axis=0))


def per_device(
    features,
    conv_one_w,
    conv_one_b,
    conv_two_w,
    conv_two_b,
    out_conv_w,
    out_conv_b,
    vgg_one_w,
    vgg_one_b,
    vgg_two_w,
    vgg_two_b,
    lin_weights,
    row_lists,
    tap_index,
    tap_weight,
    target_tiles,
):
    colour, saved = decoder_forward(
        features, conv_one_w, conv_one_b, conv_two_w, conv_two_b, out_conv_w, out_conv_b
    )
    slab = jnp.transpose(colour, (0, 2, 1))
    slab_rows, breadth = (slab.shape[0], slab.shape[2])
    row_ids = row_lists[0]
    slot_count = row_ids.shape[1]
    lists = slab[row_ids]
    from_west = from_behind(lists[0], "lon", 1)
    from_east = from_behind(lists[2], "lon", -1)
    received = jnp.stack([from_west, lists[1], from_east]).reshape(3 * slot_count, 3, breadth)
    block_index = tap_index[0] // breadth
    column = tap_index[0] % breadth
    weights_here = tap_weight[0]
    values = received[block_index, :, column]
    predicted = jnp.sum(values * weights_here[:, :, None], axis=0).T

    def local_loss(predicted_in):
        return tile_loss(
            predicted_in, target_tiles[0], vgg_one_w, vgg_one_b, vgg_two_w, vgg_two_b, lin_weights
        )

    tile_value, pullback = jax.vjp(local_loss, predicted)
    (pred_adj,) = pullback(jnp.ones_like(tile_value) * loss_scale)
    contrib = jnp.transpose(weights_here[:, None, :] * pred_adj[None], (0, 2, 1))
    buffer_adj = (
        jnp.zeros((3 * slot_count, 3, breadth), jnp.float32).at[block_index, :, column].add(contrib)
    )
    buffer_adj = buffer_adj.reshape(3, slot_count, 3, breadth)
    for_east_list = from_behind(buffer_adj[0], "lon", -1)
    for_west_list = from_behind(buffer_adj[2], "lon", 1)
    returned = jnp.stack([for_east_list, buffer_adj[1], for_west_list])
    slab_adj = (
        jnp.zeros((slab_rows, 3, breadth), jnp.float32)
        .at[row_ids.reshape(-1)]
        .add(returned.reshape(-1, 3, breadth))
    )
    colour_adj = jnp.transpose(slab_adj, (0, 2, 1))
    grad_one, grad_two, grad_out = decoder_backward(colour_adj, saved, conv_two_w, out_conv_w)
    loss, grad_one, grad_two, grad_out = lax.psum(
        (tile_value, grad_one, grad_two, grad_out), ("lon", "grp")
    )
    return (loss, grad_one, grad_two, grad_out)


def solution(mesh):
    in_specs = (
        P("grp", "lon", None),
        P(),
        P(),
        P(),
        P(),
        P(),
        P(),
        P(),
        P(),
        P(),
        P(),
        P(),
        P(("lon", "grp"), None, None),
        P(("lon", "grp"), None, None),
        P(("lon", "grp"), None, None),
        P(("lon", "grp"), None, None, None),
    )
    out_specs = (P(), P(), P(), P())
    return jax.shard_map(
        per_device, mesh=mesh, in_specs=in_specs, out_specs=out_specs, check_vma=False
    )
```

profile of v0, /device:TPU:1, one launch (start us, length us, event | category | flops | bytes accessed | tf_op | source)
XLA Modules:
  0.0 1090.0 jit_solution(7203604560761785840)
XLA Ops:
  9.4 3.7 collective-permute-start
  13.2 5.7 collective-permute-start.1
  19.7 15.4 %collective-permute-done = bf16[16,1,128]{1,2,0:T(8,128)(2,1)S(1)} collective-permute-done((bf16[16,1,128]{1,2,0:T(8,128)(2,1)S(1)}, bf16[16,1,128]{1,2,0:T(8,128)(2,1)S(1)}, u32[]{:S(2)}, u32[]{:S(2)}) %collective-permute-start) | collective-permute-done | bytes 4128 | tf_op jit(solution)/shard_map/ppermute | solution.py:19
  35.0 2.1 collective-permute-done.1
  37.3 4.6 collective-permute-start.2
  41.9 1.9 collective-permute-start.3
  44.0 3.5 collective-permute-done.3
  53.2 2.4 convolution_select_fusion.3
  59.2 2.7 collective-permute-start.4
  61.9 4.6 collective-permute-start.5
  67.0 15.9 %collective-permute-done.4 = bf16[16,1,128]{1,2,0:T(8,128)(2,1)S(1)} collective-permute-done((bf16[16,1,128]{1,2,0:T(8,128)(2,1)S(1)}, bf16[16,1,128]{1,2,0:T(8,128)(2,1)S(1)}, u32[]{:S(2)}, u32[]{:S(2)}) %collective-permute-start.4) | collective-permute-done | bytes 4128 | tf_op jit(solution)/shard_map/ppermute | solution.py:19
  82.9 2.1 collective-permute-done.5
  85.8 1.9 collective-permute-start.6
  87.7 2.4 collective-permute-start.7
  90.3 3.1 collective-permute-done.7
  93.3 2.8 maximum_bitcast_fusion.1
  103.0 2.6 copy.485
  105.6 2.5 fusion.127
  108.3 3.2 collective-permute-start.8
  111.5 4.6 collective-permute-start.9
  116.7 16.3 %collective-permute-done.8 = bf16[16,1,128]{1,2,0:T(8,128)(2,1)S(1)} collective-permute-done((bf16[16,1,128]{1,2,0:T(8,128)(2,1)S(1)}, bf16[16,1,128]{1,2,0:T(8,128)(2,1)S(1)}, u32[]{:S(2)}, u32[]{:S(2)}) %collective-permute-start.8) | collective-permute-done | bytes 4128 | tf_op jit(solution)/shard_map/ppermute | solution.py:19
  133.0 1.9 collective-permute-done.9
  135.0 1.9 collective-permute-start.10
  136.9 2.4 collective-permute-start.11
  139.3 2.3 pad_maximum_fusion
  148.2 13.1 %convolution_select_fusion.4 = f32[16,8,17,3]{1,3,2,0:T(4,128)S(1)} fusion(bf16[3,3,128,3]{2,3,1,0:T(4,128)(2,1)} %param.25, bf16[18,1,7,2,128]{4,2,3,0,1:T(8,128)(2,1)S(1)} %slice.272, bf16[18,1,8,17,128]{4,2,3,0,1:T(8,128)(2,1)S(1)} %copy.384, pred[8,17]{0,1:T(8,128)(4,1)S(1)} %copy-done.46), kind=kOutput, calls=%fused_computation.116 | convolution fusion | flops 17148288 | bytes 724360 | tf_op jit(solution)/shard_map/conv_general_dilated | solution.py:34
  163.1 2.7 collective-permute-start.12
  165.8 4.7 collective-permute-start.13
  170.5 2.4 pad_maximum_fusion.1
  173.4 353.7 %gather_fusion.1 = f32[32768,3]{1,0:T(8,128)} fusion(f32[24,3,128]{1,2,0:T(8,128)S(1)} %copy.387, s32[32768]{0:T(1024)S(1)} %bitcast.404), kind=kCustom, calls=%fused_computation.1 | custom fusion | bytes 1048576 | tf_op jit(solution)/shard_map/gather | solution.py:180
  527.1 9.8 multiply_reduce_fusion
  537.0 2.9 copy.388
  542.3 3.4 fusion.70
  551.5 4.4 fusion.58
  555.9 5.3 fusion.34
  562.9 5.4 add_maximum_fusion.1
  570.4 2.2 multiply_reduce_fusion.2
  572.6 4.8 fusion.18
  579.7 5.3 fusion.20
  585.0 4.1 copy.491
  589.1 3.6 pad.14.clone
  592.6 4.6 copy.404
  598.2 6.3 select_bitcast_fusion
  604.6 49.7 %fusion.61 = bf16[64,8,17,3]{1,3,2,0:T(4,128)(2,1)S(1)} fusion(bf16[64,1,7,1,64]{4,2,3,0,1:T(8,128)(2,1)S(1)} %get-tuple-element.18, bf16[64,1,7,1,64]{4,2,3,0,1:T(8,128)(2,1)S(1)} %get-tuple-element.17, bf16[64,1,8,17,64]{4,2,3,0,1:T(8,128)(2,1)S(1)} %select_bitcast_fusion, bf16[64,3,3,3]{0,3,2,1:T(4,128)(2,1)S(1)} %copy-done.58), kind=kOutput, calls=%fused_computation.93 | convolution fusion | flops 35993600 | bytes 1284480 | tf_op jit(solution)/shard_map/transpose(jvp())/conv_general_dilated | solution.py:45
  654.3 1.8 copy.406
  656.4 2.7 copy.408
  659.1 8.1 broadcast_multiply_fusion
  667.2 175.5 %scatter_custom_fusion.1 = f32[3,3072]{0,1:T(8,128)} fusion(s32[32768]{0:T(1024)} %bitcast.427, f32[32768,3]{1,0:T(8,128)} %bitcast.412, f32[]{:T(128)} %constant.62.clone.1), kind=kCustom, calls=%fused_computation.205 | custom fusion | flops 98304 | bytes 37376
  842.7 1.9 copy.409
  844.6 6.0 collective-permute-start.14
  850.6 2.3 pad_maximum_fusion.2
  853.5 5.3 collective-permute-done.15
  860.7 7.2 collective-permute-start.17
  873.0 5.8 collective-permute-start.18
  878.8 1.9 collective-permute-start.19
  881.2 2.5 collective-permute-done.19
  889.5 7.2 collective-permute-start.21
  897.9 12.9 %collective-permute-done.20 = bf16[16,1,128]{1,2,0:T(8,128)(2,1)S(1)} collective-permute-done((bf16[16,1,128]{1,2,0:T(8,128)(2,1)S(1)}, bf16[16,1,128]{1,2,0:T(8,128)(2,1)S(1)}, u32[]{:S(2)}, u32[]{:S(2)}) %collective-permute-start.20) | collective-permute-done | bytes 4128 | tf_op jit(solution)/shard_map/ppermute | solution.py:19
  911.0 1.9 collective-permute-start.22
  912.9 2.6 collective-permute-start.23
  929.6 67.6 %all-reduce = (f32[]{:T(128)}, f32[3,3,128,3]{2,3,1,0:T(4,128)}) all-reduce(f32[]{:T(128)S(6)} %div.80, f32[3,3,128,3]{2,3,1,0:T(4,128)S(1)} %bitcast.428), channel_id=1, replica_groups=mesh['lon'=32,'grp'=4] {'lon','grp'}, use_global_device_ids=true, to_apply=%region_4.5 | all-reduce | flops 3457 | bytes 27656 | tf_op jit(solution)/shard_map/psum | solution.py:205
  997.3 81.9 %all-reduce.4.cloned.1.call-done = (f32[3,3,128,128]{3,2,1,0:T(8,128)}, f32[3,3,128,128]{3,2,1,0:T(8,128)}) async-done(((f32[3,3,128,128]{3,2,1,0:T(8,128)}, f32[3,3,128,128]{3,2,1,0:T(8,128)}), (f32[3,3,128,128]{3,2,1,0:T(8,128)}, f32[3,3,128,128]{3,2,1,0:T(8,128)})) %all-reduce.4.cloned.1.call-update) | async-done | bytes 1179664 | tf_op jit(solution)/shard_map/psum | solution.py:205
  1079.1 1.9 copy.531
  1081.0 1.9 copy.532
  (274 shorter events, 74.1 us)
Async XLA Ops:
  7.2 93.1 %copy-start = (bf16[3,3,128,128]{3,2,1,0:T(8,128)(2,1)S(1)}, bf16[3,3,128,128]{3,2,1,0:T(8,128)(2,1)}, u32[]{:S(2)}) copy-start(bf16[3,3,128,128]{3,2,1,0:T(8,128)(2,1)} %param.23) | copy-start | bytes 884740
  7.2 12.1 %copy-start.54 = (s32[2]{0:T(128)S(1)}, s32[2]{0:T(128)}, u32[]{:S(2)}) copy-start(s32[2]{0:T(128)} %constant.73) | copy-start | bytes 28
  7.2 11.7 %copy-start.42 = (s32[1,4,8192]{2,1,0:T(4,128)S(1)}, s32[1,4,8192]{2,1,0:T(4,128)}, u32[]{:S(2)}) copy-start(s32[1,4,8192]{2,1,0:T(4,128)} %param.33) | copy-start | bytes 393220
  7.2 1071.9 %all-reduce.4.cloned.1.call-start = ((), (), s32[]{:S(2)}) async-start(), calls=%async_computation | async-start | bytes 2359296 | tf_op jit(solution)/shard_map/psum | solution.py:205
  8.6 10.7 copy-start.55
  8.9 130.4 %copy-start.1 = (bf16[16,128,128]{1,2,0:T(8,128)(2,1)}, bf16[16,128,128]{1,2,0:T(8,128)(2,1)S(1)}, u32[]{:S(2)}) copy-start(bf16[16,128,128]{1,2,0:T(8,128)(2,1)S(1)} %fusion.113) | copy-start | bytes 1572868
  8.9 34.9 %copy-start.47 = (f32[64]{0:T(128)S(1)}, f32[64]{0:T(128)}, u32[]{:S(2)}) copy-start(f32[64]{0:T(128)} %param.31) | copy-start | bytes 772
  9.0 34.9 %copy-start.44 = (s32[1,3,8]{2,0,1:T(1,128)S(1)}, s32[1,3,8]{2,0,1:T(1,128)}, u32[]{:S(2)}) copy-start(s32[1,3,8]{2,0,1:T(1,128)} %param.32) | copy-start | bytes 292
  9.4 25.6 %collective-permute-start = (bf16[16,1,128]{1,2,0:T(8,128)(2,1)S(1)}, bf16[16,1,128]{1,2,0:T(8,128)(2,1)S(1)}, u32[]{:S(2)}, u32[]{:S(2)}) collective-permute-start(bf16[16,1,128]{1,2,0:T(8,128)(2,1)S(1)} %get-tuple-element.43), channel_id=1, source_target_pairs={{0,4},{4,8},{8,12},{12,16},{16,20},{20,24},{24,28},{28,32},{32,36}... | collective-permute-start | bytes 12296 | tf_op jit(solution)/shard_map/ppermute | solution.py:19
  13.2 24.0 %collective-permute-start.1 = (bf16[16,1,128]{1,2,0:T(8,128)(2,1)S(1)}, bf16[16,1,128]{1,2,0:T(8,128)(2,1)S(1)}, u32[]{:S(2)}, u32[]{:S(2)}) collective-permute-start(bf16[16,1,128]{1,2,0:T(8,128)(2,1)S(1)} %get-tuple-element.44), channel_id=1, source_target_pairs={{4,0},{8,4},{12,8},{16,12},{20,16},{24,20},{28,24},{32,28},{36,32}... | collective-permute-start | bytes 12296 | tf_op jit(solution)/shard_map/ppermute | solution.py:21
  35.0 14.1 %copy-start.9 = (bf16[16,1,128]{1,2,0:T(8,128)(2,1)}, bf16[16,1,128]{1,2,0:T(8,128)(2,1)S(1)}, u32[]{:S(2)}) copy-start(bf16[16,1,128]{1,2,0:T(8,128)(2,1)S(1)} %collective-permute-done) | copy-start | bytes 12292
  37.2 102.1 %copy-start.7 = (bf16[16,1,128]{1,2,0:T(8,128)(2,1)}, bf16[16,1,128]{1,2,0:T(8,128)(2,1)S(1)}, u32[]{:S(2)}) copy-start(bf16[16,1,128]{1,2,0:T(8,128)(2,1)S(1)} %collective-permute-done.1) | copy-start | bytes 12292
  37.3 6.7 collective-permute-start.2
  41.9 5.6 collective-permute-start.3
  47.5 3.3 copy-start.36
  55.9 2.7 copy-start.49
  58.6 26.6 %copy-start.5 = (f32[16,1,128,128]{2,3,0,1:T(8,128)}, f32[16,1,128,128]{2,3,0,1:T(8,128)S(1)}, u32[]{:S(2)}) copy-start(f32[16,1,128,128]{2,3,0,1:T(8,128)S(1)} %copy.484) | copy-start | bytes 3145732
  58.9 111.6 %copy-start.3 = (bf16[16,128,128]{1,2,0:T(8,128)(2,1)}, bf16[16,128,128]{1,2,0:T(8,128)(2,1)S(1)}, u32[]{:S(2)}) copy-start(bf16[16,128,128]{1,2,0:T(8,128)(2,1)S(1)} %fusion.119) | copy-start | bytes 1572868
  59.2 23.7 %collective-permute-start.4 = (bf16[16,1,128]{1,2,0:T(8,128)(2,1)S(1)}, bf16[16,1,128]{1,2,0:T(8,128)(2,1)S(1)}, u32[]{:S(2)}, u32[]{:S(2)}) collective-permute-start(bf16[16,1,128]{1,2,0:T(8,128)(2,1)S(1)} %get-tuple-element.41), channel_id=1, source_target_pairs={{0,4},{4,8},{8,12},{12,16},{16,20},{20,24},{24,28},{28,32},{32,36}... | collective-permute-start | bytes 12296 | tf_op jit(solution)/shard_map/ppermute | solution.py:19
  61.9 23.2 %collective-permute-start.5 = (bf16[16,1,128]{1,2,0:T(8,128)(2,1)S(1)}, bf16[16,1,128]{1,2,0:T(8,128)(2,1)S(1)}, u32[]{:S(2)}, u32[]{:S(2)}) collective-permute-start(bf16[16,1,128]{1,2,0:T(8,128)(2,1)S(1)} %get-tuple-element.42), channel_id=1, source_target_pairs={{4,0},{8,4},{12,8},{16,12},{20,16},{24,20},{28,24},{32,28},{36,32}... | collective-permute-start | bytes 12296 | tf_op jit(solution)/shard_map/ppermute | solution.py:21
  82.9 4.9 copy-start.15
  85.8 4.4 collective-permute-start.6
  87.7 5.6 collective-permute-start.7
  90.3 7.6 copy-start.38
  93.3 4.6 copy-start.40
  101.9 3.7 copy-start.23
  102.0 3.6 copy-start.56
  108.1 31.2 %copy-start.10 = (bf16[16,1,128]{1,2,0:T(8,128)(2,1)S(1)}, bf16[16,1,128]{1,2,0:T(8,128)(2,1)}, u32[]{:S(2)}) copy-start(bf16[16,1,128]{1,2,0:T(8,128)(2,1)} %copy-done.9) | copy-start | bytes 12292
  108.1 31.2 %copy-start.37 = (bf16[1,130,128]{1,2,0:T(8,128)(2,1)S(1)}, bf16[1,130,128]{1,2,0:T(8,128)(2,1)}, u32[]{:S(2)}) copy-start(bf16[1,130,128]{1,2,0:T(8,128)(2,1)} %copy-done.36) | copy-start | bytes 99844
  108.3 24.6 %collective-permute-start.8 = (bf16[16,1,128]{1,2,0:T(8,128)(2,1)S(1)}, bf16[16,1,128]{1,2,0:T(8,128)(2,1)S(1)}, u32[]{:S(2)}, u32[]{:S(2)}) collective-permute-start(bf16[16,1,128]{1,2,0:T(8,128)(2,1)S(1)} %get-tuple-element.39), channel_id=1, source_target_pairs={{0,4},{4,8},{8,12},{12,16},{16,20},{20,24},{24,28},{28,32},{32,36}... | collective-permute-start | bytes 12296 | tf_op jit(solution)/shard_map/ppermute | solution.py:19
  111.5 23.3 %collective-permute-start.9 = (bf16[16,1,128]{1,2,0:T(8,128)(2,1)S(1)}, bf16[16,1,128]{1,2,0:T(8,128)(2,1)S(1)}, u32[]{:S(2)}, u32[]{:S(2)}) collective-permute-start(bf16[16,1,128]{1,2,0:T(8,128)(2,1)S(1)} %get-tuple-element.40), channel_id=1, source_target_pairs={{4,0},{8,4},{12,8},{16,12},{20,16},{24,20},{28,24},{32,28},{36,32}... | collective-permute-start | bytes 12296 | tf_op jit(solution)/shard_map/ppermute | solution.py:21
  133.0 9.5 copy-start.20
  134.8 7.6 copy-start.18
  135.0 6.7 collective-permute-start.10
  136.9 5.6 collective-permute-start.11
  148.1 22.4 %copy-start.13 = (bf16[16,1,128]{1,2,0:T(8,128)(2,1)S(1)}, bf16[16,1,128]{1,2,0:T(8,128)(2,1)}, u32[]{:S(2)}) copy-start(bf16[16,1,128]{1,2,0:T(8,128)(2,1)} %copy-done.12) | copy-start | bytes 12292
  148.1 22.4 %copy-start.16 = (bf16[16,1,128]{1,2,0:T(8,128)(2,1)S(1)}, bf16[16,1,128]{1,2,0:T(8,128)(2,1)}, u32[]{:S(2)}) copy-start(bf16[16,1,128]{1,2,0:T(8,128)(2,1)} %copy-done.15) | copy-start | bytes 12292
  148.1 22.4 %copy-start.39 = (bf16[1,130,128]{1,2,0:T(8,128)(2,1)S(1)}, bf16[1,130,128]{1,2,0:T(8,128)(2,1)}, u32[]{:S(2)}) copy-start(bf16[1,130,128]{1,2,0:T(8,128)(2,1)} %copy-done.38) | copy-start | bytes 99844
  148.2 22.4 %copy-start.41 = (bf16[1,130,128]{1,2,0:T(8,128)(2,1)S(1)}, bf16[1,130,128]{1,2,0:T(8,128)(2,1)}, u32[]{:S(2)}) copy-start(bf16[1,130,128]{1,2,0:T(8,128)(2,1)} %copy-done.40) | copy-start | bytes 99844
  163.1 9.8 collective-permute-start.12
  165.8 7.1 collective-permute-start.13
  173.4 353.7 %copy-start.35 = (f32[1,4,8192]{2,1,0:T(4,128)S(1)}, f32[1,4,8192]{2,1,0:T(4,128)}, u32[]{:S(2)}) copy-start(f32[1,4,8192]{2,1,0:T(4,128)} %param.34) | copy-start | bytes 393220
  537.0 2.9 copy-start.43
  537.0 2.9 copy-start.48
  537.0 2.9 copy-start.53
  539.8 2.4 copy-start.58
  542.3 3.4 copy-start.51
  551.5 4.5 copy-start.57
  667.2 183.4 %copy-start.19 = (bf16[16,1,128]{1,2,0:T(8,128)(2,1)S(1)}, bf16[16,1,128]{1,2,0:T(8,128)(2,1)}, u32[]{:S(2)}) copy-start(bf16[16,1,128]{1,2,0:T(8,128)(2,1)} %copy-done.18) | copy-start | bytes 12292
  667.2 183.4 %copy-start.21 = (bf16[16,1,128]{1,2,0:T(8,128)(2,1)S(1)}, bf16[16,1,128]{1,2,0:T(8,128)(2,1)}, u32[]{:S(2)}) copy-start(bf16[16,1,128]{1,2,0:T(8,128)(2,1)} %copy-done.20) | copy-start | bytes 12292
  844.6 14.3 %copy-start.52 = (s32[24]{0:T(128)S(1)}, s32[24]{0:T(128)}, u32[]{:S(2)}) copy-start(s32[24]{0:T(128)} %fusion.211) | copy-start | bytes 292
  844.6 8.9 collective-permute-start.14
  850.6 8.3 collective-permute-start.15
  860.7 12.2 %collective-permute-start.16 = (bf16[16,1,3]{1,2,0:T(4,128)(2,1)S(1)}, bf16[16,1,3]{1,2,0:T(4,128)(2,1)S(1)}, u32[]{:S(2)}, u32[]{:S(2)}) collective-permute-start(bf16[16,1,3]{1,2,0:T(4,128)(2,1)S(1)} %get-tuple-element.53), channel_id=1, source_target_pairs={{0,4},{4,8},{8,12},{12,16},{16,20},{20,24},{24,28},{28,32},{32,36}... | collective-permute-start | bytes 296 | tf_op jit(solution)/shard_map/ppermute | solution.py:19
  860.7 12.2 %collective-permute-start.17 = (bf16[16,1,3]{1,2,0:T(4,128)(2,1)S(1)}, bf16[16,1,3]{1,2,0:T(4,128)(2,1)S(1)}, u32[]{:S(2)}, u32[]{:S(2)}) collective-permute-start(bf16[16,1,3]{1,2,0:T(4,128)(2,1)S(1)} %get-tuple-element.54), channel_id=1, source_target_pairs={{4,0},{8,4},{12,8},{16,12},{20,16},{24,20},{28,24},{32,28},{36,32}... | collective-permute-start | bytes 296 | tf_op jit(solution)/shard_map/ppermute | solution.py:21
  870.7 13.9 %copy-start.59 = (bf16[3,3,128,3]{2,3,1,0:T(4,128)(2,1)S(1)}, bf16[3,3,128,3]{2,3,1,0:T(4,128)(2,1)}, u32[]{:S(2)}) copy-start(bf16[3,3,128,3]{2,3,1,0:T(4,128)(2,1)} %param.25) | copy-start | bytes 20740
  873.0 8.2 collective-permute-start.18
  878.8 4.9 collective-permute-start.19
  888.0 8.7 copy-start.14
  888.8 8.5 copy-start.30
  889.5 21.4 %collective-permute-start.20 = (bf16[16,1,128]{1,2,0:T(8,128)(2,1)S(1)}, bf16[16,1,128]{1,2,0:T(8,128)(2,1)S(1)}, u32[]{:S(2)}, u32[]{:S(2)}) collective-permute-start(bf16[16,1,128]{1,2,0:T(8,128)(2,1)S(1)} %get-tuple-element.37), channel_id=1, source_target_pairs={{0,4},{4,8},{8,12},{12,16},{16,20},{20,24},{24,28},{28,32},{32,36}... | collective-permute-start | bytes 12296 | tf_op jit(solution)/shard_map/ppermute | solution.py:19
  889.5 21.3 %collective-permute-start.21 = (bf16[16,1,128]{1,2,0:T(8,128)(2,1)S(1)}, bf16[16,1,128]{1,2,0:T(8,128)(2,1)S(1)}, u32[]{:S(2)}, u32[]{:S(2)}) collective-permute-start(bf16[16,1,128]{1,2,0:T(8,128)(2,1)S(1)} %get-tuple-element.38), channel_id=1, source_target_pairs={{4,0},{8,4},{12,8},{16,12},{20,16},{24,20},{28,24},{32,28},{36,32}... | collective-permute-start | bytes 12296 | tf_op jit(solution)/shard_map/ppermute | solution.py:21
  911.0 4.9 collective-permute-start.22
  912.9 5.6 collective-permute-start.23
  (21 other events, 29.4 us)
Sparse Core Ops, SparseCore 0:
  928.8 150.2 all-reduce.3
where the time goes:
time: 1100 us; the launch traced here: 1090 us
  local copies, waits for them, and re-layouts  424 us (39%)
  other arithmetic  230 us (21%)
  waiting for transfers between devices  166 us (15%)
  matrix products  107 us (10%)
  starting transfers between devices  79.7 us (7%)
  blocking collectives  67.6 us (6%)
  between operations  16.4 us (1%)
    gather x1, local copies, waits for them, and re-layouts, per_device(): values = received[block_index, :, column]  354 us
    unnamed x6, other arithmetic  176 us
    psum x1, waiting for transfers between devices, per_device(): lax.psum((tile_value, grad_one, grad_two, grad_out), ('lon', 'grp'))  81.9 us
    conv_general_dilated x6, matrix products, conv_same(): lax.conv_general_dilated(picture[None], weight, (1, 1), 'SAME', dimension...  74.5 us
    psum x1, blocking collectives, per_device(): lax.psum((tile_value, grad_one, grad_two, grad_out), ('lon', 'grp'))  67.6 us
    ppermute x10, waiting for transfers between devices, extended(): lax.ppermute(tail, axis, [(i, (i + 1) % count) for i in range(ends)])  60.5 us
    ppermute x10, starting transfers between devices, extended(): lax.ppermute(head, axis, [((i + 1) % count, i) for i in range(ends)])  40.4 us
    unnamed x135, local copies, waits for them, and re-layouts  30.8 us
  transfers between devices with their start and end apart: 25, of which 14 were waited for; matrix products, arithmetic and copies ran while one was open for 2% of the time, Pallas kernels for 0%

commit v1 on v0

v1 whole, which is shorter than its diff:
```python
import jax
import jax.numpy as jnp
from jax import lax
from jax.experimental import pallas as pl
from jax.experimental.pallas import tpu as pltpu
from jax.sharding import PartitionSpec as P

OFFSET = (-0.03, -0.088, -0.188)
SPREAD = (0.458, 0.448, 0.45)
LOSS_SCALE = 64.0

CH = 128
VW = 64
ROWS = 16
COLS = 128
WIDE = 160
TROWS = 64
PIX = TROWS * 128
BF = jnp.bfloat16
F32 = jnp.float32
MESH = pl.DeviceIdType.MESH

AROUND = ((-1, -1), (-1, 0), (-1, 1), (0, -1), (0, 1), (1, -1), (1, 0), (1, 1))


def dot(a, b, ca=1, cb=0):
    return lax.dot_general(a, b, (((ca,), (cb,)), ((), ())), preferred_element_type=F32)


def span(start, size, unit):
    if isinstance(start, int):
        return pl.ds(start, size)
    return pl.ds(pl.multiple_of(start, unit), size)


def ext(delta, low, high):
    return low if delta < 0 else high


def conv_rows(src, weight, r, n, last=0):
    lhs = jnp.concatenate(
        [src[pl.ds(r + a, n)].reshape(n * WIDE, CH) for a in range(3)], axis=1
    )
    z = dot(lhs, weight, 1, last)
    return (
        pltpu.roll(z[:, :CH], 1, 0)
        + z[:, CH : 2 * CH]
        + pltpu.roll(z[:, 2 * CH :], n * WIDE - 1, 0)
    )


def act_slope(hidden):
    h = hidden.astype(F32)
    s = jax.nn.sigmoid(h)
    return (h * s).astype(BF), s * (1.0 + h * (1.0 - s))


def lane_masks(n):
    col = lax.broadcasted_iota(jnp.int32, (1, 128), 1)
    return col > 0, col < 127


def shift_store(ref, y, row0, n):
    first, last = lane_masks(n)
    for r in range(n):
        part = y[:, r * 128 : (r + 1) * 128]
        at = span((row0 + r + 1) * 128, 128, 128)
        ref[0, :, at] = jnp.where(first, pltpu.roll(part, 1, 1), 0.0).astype(BF)
        ref[1, :, at] = part.astype(BF)
        ref[2, :, at] = jnp.where(last, pltpu.roll(part, 127, 1), 0.0).astype(BF)


def per_channel(values):
    row = lax.broadcasted_iota(jnp.int32, (8, 1), 0)
    out = jnp.full((8, 1), values[2], F32)
    out = jnp.where(row == 0, values[0], out)
    return jnp.where(row == 1, values[1], out)


def store_scaled(zs, colours, row0, n):
    row = lax.broadcasted_iota(jnp.int32, (8, 1), 0)
    z = jnp.where(row < 3, (colours - per_channel(OFFSET)) / per_channel(SPREAD), 0.0)
    first, last = lane_masks(n)
    for r in range(n):
        part = z[:, r * 128 : (r + 1) * 128]
        stack = jnp.concatenate(
            [
                jnp.where(first, pltpu.roll(part, 1, 1), 0.0),
                part,
                jnp.where(last, pltpu.roll(part, 127, 1), 0.0),
                jnp.zeros_like(part),
            ],
            axis=0,
        )
        zs[:, span((row0 + r + 1) * 128, 128, 128)] = stack.astype(BF)


def vgg_first(zs, fs, v1, v1b, n):
    @pl.loop(0, TROWS // n)
    def _(k):
        r0 = k * n
        rhs = jnp.concatenate(
            [zs[:, span((r0 + a) * 128, n * 128, 128)] for a in range(3)], axis=0
        )
        y = jnp.maximum(dot(v1, rhs) + v1b, 0.0)
        shift_store(fs, y, r0, n)


def nine_taps(ref, r0, n):
    return jnp.concatenate(
        [ref[b, :, span((r0 + a) * 128, n * 128, 128)] for a in range(3) for b in range(3)], axis=0
    )


def inv_norm(f):
    return lax.rsqrt(jnp.sum(f * f, axis=0, keepdims=True) + 1e-05)


def kernel(
    feat, w1, b1, w2, b2, wo, bo, v1w, v1b, v2w, v2b, lin, rows_ref, tap_i, tap_w, target,
    grads, loss_out,
    f_ref, a0, a1, a2, s1, s2, w1c, w2c, w2f, c_own, c_near, hot, al, ar, v1f, v2c, v2t,
    zs, fs, gs, unit_t, y_ref, tb, pb, ca, ca_near, own_e, all_e, d2, d1, t0, t1, loss_acc, wof,
    halo_send, halo_recv, col_send, col_recv, tab_send, tab_recv, adj_send, adj_recv,
):
    lon, grp = lax.axis_index("lon"), lax.axis_index("grp")
    n_lon, n_grp = lax.axis_size("lon"), lax.axis_size("grp")

    def near(dl, dg):
        return (lax.rem(lon + dl + n_lon, n_lon), lax.rem(grp + dg + n_grp, n_grp))

    barrier = pltpu.get_barrier_semaphore()
    for dl, dg in AROUND:
        pl.semaphore_signal(barrier, inc=1, device_id=near(dl, dg), device_id_type=MESH)

    for a in range(3):
        for b in range(3):
            rows, cols = slice(a * CH, (a + 1) * CH), slice(b * CH, (b + 1) * CH)
            w1c[rows, cols] = w1[a, b]
            w2c[rows, cols] = w2[a, b]
            w2f[cols, rows] = w2[2 - a, 2 - b]
    v1f[...] = jnp.zeros_like(v1f)
    wof[...] = jnp.zeros_like(wof)
    for a in range(3):
        for b in range(3):
            for c in range(3):
                v1f[a * 32 + b * 8 + c : a * 32 + b * 8 + c + 1, :] = v1w[c, a, b : b + 1].astype(F32)
            wof[a, b * 8 : b * 8 + 3, :] = wo[a, b].astype(F32)
            v2c[:, (a * 3 + b) * VW : (a * 3 + b + 1) * VW] = v2w[a, b]
            v2t[:, (a * 3 + b) * VW : (a * 3 + b + 1) * VW] = (
                v2w[2 - a, 2 - b].astype(F32).T.astype(BF)
            )
    v1 = v1f[...].T.astype(BF)
    v1b_col = v1b[...].reshape(VW, 1)
    v2b_col = v2b[...].reshape(VW, 1)
    lin_col = lin[...].reshape(VW, 1)

    zs[:, 0:128] = jnp.zeros((32, 128), BF)
    zs[:, PIX + 128 :] = jnp.zeros((32, 128), BF)
    for ref in (fs, gs):
        ref[:, :, 0:128] = jnp.zeros((3, VW, 128), BF)
        ref[:, :, PIX + 128 :] = jnp.zeros((3, VW, 128), BF)
    y_ref[:, 0:128] = jnp.zeros((72, 128), F32)
    y_ref[:, PIX + 128 :] = jnp.zeros((72, 128), F32)
    pb[:, :, 0:8, :] = jnp.zeros((3, 3, 8, 128), F32)
    pb[:, :, 16:24, :] = jnp.zeros((3, 3, 8, 128), F32)
    own_e[...] = jnp.zeros_like(own_e)
    all_e[...] = jnp.zeros_like(all_e)

    pl.semaphore_wait(barrier, len(AROUND))
    take_r = {-1: pl.ds(0, 3), 0: pl.ds(0, ROWS), 1: pl.ds(ROWS - 3, 3)}
    take_c = {-1: pl.ds(0, 16), 0: pl.ds(0, COLS), 1: pl.ds(COLS - 16, 16)}
    land_r = {-1: pl.ds(ROWS + 3, 3), 0: pl.ds(3, ROWS), 1: pl.ds(0, 3)}
    land_c = {-1: pl.ds(COLS + 16, 16), 0: pl.ds(16, COLS), 1: pl.ds(0, 16)}
    halo = []
    for i, (dl, dg) in enumerate(AROUND):
        copy = pltpu.make_async_remote_copy(
            src_ref=feat.at[take_r[dg], take_c[dl]],
            dst_ref=f_ref.at[land_r[dg], land_c[dl]],
            send_sem=halo_send.at[i],
            recv_sem=halo_recv.at[i],
            device_id=near(dl, dg),
            device_id_type=MESH,
        )
        copy.start()
        halo.append(copy)
    f_ref[3 : 3 + ROWS, 16 : 16 + COLS, :] = feat[...]

    for r in range(TROWS):
        tgt = target[:, r, :].astype(F32)
        unit_t[0:8, r * 128 : (r + 1) * 128] = jnp.concatenate(
            [tgt, jnp.zeros((5, 128), F32)], axis=0
        )

    @pl.loop(0, 8)
    def _(k):
        store_scaled(zs, unit_t[0:8, span(k * 1024, 1024, 128)], k * 8, 8)

    vgg_first(zs, fs, v1, v1b_col, 4)

    @pl.loop(0, TROWS // 4)
    def _(k):
        f = jnp.maximum(dot(v2c[...], nine_taps(fs, k * 4, 4)) + v2b_col, 0.0)
        unit_t[:, span(k * 512, 512, 128)] = f * inv_norm(f)

    @pl.loop(0, 8)
    def _(k):
        at = span(k * 1024, 1024, 128)
        index = tap_i[:, at]
        weight = tap_w[:, at]
        column = lax.shift_left(lax.shift_right_logical(index, 10), 7) + jnp.bitwise_and(index, 127)
        slot = jnp.bitwise_and(lax.shift_right_logical(index, 7), 7)
        left = jnp.min(column, axis=0, keepdims=True)
        top = jnp.min(slot, axis=0, keepdims=True)
        is_left, is_top = column == left, slot == top

        def corner(cond):
            return jnp.sum(jnp.where(cond, weight, 0.0), axis=0, keepdims=True)

        not_left, not_top = jnp.logical_not(is_left), jnp.logical_not(is_top)
        w_tl, w_tr = corner(is_top & is_left), corner(is_top & not_left)
        w_bl, w_br = corner(not_top & is_left), corner(not_top & not_left)
        j = lax.broadcasted_iota(jnp.int32, (8, 1024), 0)
        on_top, on_next = j == top, j == top + 1
        al[:, at] = jnp.where(on_top, w_tl, jnp.where(on_next, w_bl, 0.0))
        ar[:, at] = jnp.where(on_top, w_tr, jnp.where(on_next, w_br, 0.0))
        x = lax.broadcasted_iota(jnp.int32, (384, 1024), 0)
        hot[:, at] = jnp.where(x == left, 1.0, 0.0).astype(BF)

    for copy in halo:
        copy.wait()
    north, south = grp == 0, grp == n_grp - 1

    @pl.loop(0, ROWS + 6)
    def _(r):
        a0[r] = act_slope(f_ref[r])[0]

    def clear(ref, rows):
        @pl.when(north)
        def _():
            ref[0:rows] = jnp.zeros((rows, WIDE, CH), BF)

        @pl.when(south)
        def _():
            ref[ref.shape[0] - rows :] = jnp.zeros((rows, WIDE, CH), BF)

    clear(a0, 3)

    @pl.loop(0, 5)
    def _(k):
        r = k * 4
        h = (conv_rows(a0, w1c[...], r, 4) + b1[...]).astype(BF)
        act, slope = act_slope(h)
        a1[pl.ds(r, 4)] = act.reshape(4, WIDE, CH)
        s1[pl.ds(r, 4)] = slope.reshape(4, WIDE, CH)

    clear(a1, 2)

    @pl.loop(0, 6)
    def _(k):
        r = k * 3
        f = f_ref[pl.ds(r + 2, 3)].reshape(3 * WIDE, CH).astype(F32)
        h = (f + conv_rows(a1, w2c[...], r, 3) + b2[...]).astype(BF)
        act, slope = act_slope(h)
        a2[pl.ds(r, 3)] = act.reshape(3, WIDE, CH)
        s2[pl.ds(r, 3)] = slope.reshape(3, WIDE, CH)

    clear(a2, 1)

    wo_cat = jnp.concatenate([wof[a] for a in range(3)], axis=1).astype(BF)
    for r in range(ROWS):
        rhs = jnp.concatenate([a2[r + a] for a in range(3)], axis=1)
        z = dot(wo_cat, rhs, 1, 1)
        colour = z[0:8, 15 : 15 + COLS] + z[8:16, 16 : 16 + COLS] + z[16:24, 17 : 17 + COLS]
        for c in range(3):
            c_own[c, r : r + 1, :] = colour[c : c + 1] + bo[c]

    colours = []
    for i, dl in enumerate((-1, 1)):
        copy = pltpu.make_async_remote_copy(
            src_ref=c_own,
            dst_ref=c_near.at[1 - i],
            send_sem=col_send.at[i],
            recv_sem=col_recv.at[1 - i],
            device_id=near(dl, 0),
            device_id_type=MESH,
        )
        copy.start()
        colours.append(copy)

    for act, turned, first_row in ((a0, t0, 2), (a1, t1, 1)):

        @pl.loop(0, ROWS + 2)
        def _(r, act=act, turned=turned, first_row=first_row):
            block = act[r + first_row].astype(F32).T
            at = span(r * 128, 128, 128)
            for b in range(3):
                turned[b, :, at] = block[:, 15 + b : 15 + b + COLS].astype(BF)

    for copy in colours:
        copy.wait()

    start = rows_ref[0, 1, 0]
    slabs = (c_near.at[0], c_own, c_near.at[1])
    table = jnp.concatenate(
        [
            jnp.concatenate([slab[c, pl.ds(start, 8), :] for c in range(3)], axis=0)
            for slab in slabs
        ],
        axis=1,
    )
    table = jnp.concatenate([table, pltpu.roll(table, 383, 1)], axis=0)
    table_hi = table.astype(BF)
    table_lo = (table - table_hi.astype(F32)).astype(BF)
    table = jnp.concatenate([table_hi, table_lo], axis=0)

    @pl.loop(0, 8)
    def _(k):
        at = span(k * 1024, 1024, 128)
        got = dot(table, hot[:, at])
        got = got[0:48] + got[48:96]
        w_left, w_right = al[:, at], ar[:, at]
        picture = [
            jnp.sum(
                got[c * 8 : c * 8 + 8] * w_left + got[24 + c * 8 : 32 + c * 8] * w_right,
                axis=0,
                keepdims=True,
            )
            for c in range(3)
        ]
        picture = jnp.concatenate(picture + [jnp.zeros((5, 1024), F32)], axis=0)
        store_scaled(zs, picture, k * 8, 8)

    vgg_first(zs, fs, v1, v1b_col, 4)
    loss_acc[...] = jnp.zeros_like(loss_acc)

    @pl.loop(0, TROWS // 4)
    def _(k):
        f = jnp.maximum(dot(v2c[...], nine_taps(fs, k * 4, 4)) + v2b_col, 0.0)
        inv = inv_norm(f)
        u = f * inv
        diff = u - unit_t[:, span(k * 512, 512, 128)]
        weighted = lin_col * diff
        loss_acc[...] += jnp.sum(weighted * diff, axis=0, keepdims=True)
        g = weighted * (2.0 * LOSS_SCALE / PIX)
        g = inv * (g - u * jnp.sum(g * u, axis=0, keepdims=True))
        shift_store(gs, jnp.where(f > 0.0, g, 0.0), k * 4, 4)

    loss = jnp.sum(loss_acc[...], axis=1, keepdims=True) * (1.0 / PIX)
    loss_out[...] = jnp.broadcast_to(loss, (8, 128))

    v1_back = jnp.concatenate(
        [
            v1f[(2 - a) * 32 + (2 - b) * 8 : (2 - a) * 32 + (2 - b) * 8 + 8, :]
            for b in range(3)
            for a in range(3)
        ],
        axis=0,
    ).astype(BF)

    @pl.loop(0, TROWS // 4)
    def _(k):
        g = dot(v2t[...], nine_taps(gs, k * 4, 4)).astype(BF)
        at = span((k * 4 + 1) * 128, 512, 128)
        g = jnp.where(fs[1, :, at] > 0, g, jnp.zeros_like(g))
        y_ref[:, at] = dot(v1_back, g)

    def table_adjoint(k, acc):
        at = span(k * 1024, 1024, 128)
        part = []
        for b in range(3):
            part.append(
                sum(
                    y_ref[(b * 3 + a) * 8 : (b * 3 + a) * 8 + 8, span((k * 8 + a) * 128, 1024, 128)]
                    for a in range(3)
                )
            )
        col = jnp.bitwise_and(lax.broadcasted_iota(jnp.int32, (8, 1024), 1), 127)
        dz = (
            jnp.where(col > 0, pltpu.roll(part[0], 1, 1), 0.0)
            + part[1]
            + jnp.where(col < 127, pltpu.roll(part[2], 1023, 1), 0.0)
        )
        dz = dz.astype(BF).astype(F32) / per_channel(SPREAD)
        spread = jnp.concatenate(
            [w[:, at] * dz[c : c + 1] for w in (al, ar) for c in range(3)], axis=0
        )
        hi = spread.astype(BF)
        lo = (spread - hi.astype(F32)).astype(BF)
        return acc + dot(jnp.concatenate([hi, lo], axis=0), hot[:, at], 1, 1)

    acc = lax.fori_loop(0, 8, table_adjoint, jnp.zeros((96, 384), F32))
    acc = acc[0:48] + acc[48:96]
    adjoint = acc[0:24] + pltpu.roll(acc[24:48], 1, 1)
    for k in range(3):
        for c in range(3):
            tb[k, c] = adjoint[c * 8 : c * 8 + 8, k * 128 : (k + 1) * 128]
    pb[1, :, 8:16, :] = tb[1]

    returned = []
    for i, (k, dl) in enumerate(((0, -1), (2, 1))):
        copy = pltpu.make_async_remote_copy(
            src_ref=tb.at[k],
            dst_ref=pb.at[k, :, pl.ds(8, 8), :],
            send_sem=tab_send.at[i],
            recv_sem=tab_recv.at[i],
            device_id=near(dl, 0),
            device_id_type=MESH,
        )
        copy.start()
        returned.append(copy)
    for copy in returned:
        copy.wait()

    for c in range(3):
        placed = sum(pb[k, c, pl.ds(8 - rows_ref[0, k, 0], ROWS), :] for k in range(3))
        ca[c] = placed.astype(BF)

    exchanged = []
    for i, (dl, dg) in enumerate(AROUND):
        copy = pltpu.make_async_remote_copy(
            src_ref=ca,
            dst_ref=ca_near.at[7 - i],
            send_sem=adj_send.at[i],
            recv_sem=adj_recv.at[7 - i],
            device_id=near(dl, dg),
            device_id_type=MESH,
        )
        copy.start()
        exchanged.append(copy)

    def taps_of(target_e, c, field):
        for b in range(3):
            moved = pltpu.roll(field, 384 - (111 + 2 - b), 1)[:, 0:256]
            target_e[:, b * 8 + c, :] = moved

    def patches(source_e, r):
        return jnp.concatenate([source_e[r + a] for a in range(3)], axis=0)[:, :WIDE].astype(BF)

    rows2 = jnp.zeros((2, 384), F32)
    own = [ca[c].astype(F32) for c in range(3)]
    for c in range(3):
        side = jnp.zeros((ROWS, 128), F32)
        middle = jnp.concatenate([side, own[c], side], axis=1)
        taps_of(own_e, c, jnp.concatenate([rows2, middle, rows2], axis=0))
    grad_out = jnp.zeros((96, CH), F32)
    for r in range(ROWS + 2):
        grad_out += dot(patches(own_e, r), a2[r])
    for a in range(3):
        base = 18 * CH + (2 - a) * 32
        grads[base : base + 32, :] = grad_out[a * 32 : a * 32 + 32]

    for copy in exchanged:
        copy.wait()
    at_of = {delta: i for i, delta in enumerate(AROUND)}
    has_north = jnp.where(north, 0.0, 1.0)
    has_south = jnp.where(south, 0.0, 1.0)
    for c in range(3):

        def line(dg):
            parts = [
                own[c] if (dl, dg) == (0, 0) else ca_near[at_of[(dl, dg)], c].astype(F32)
                for dl in (-1, 0, 1)
            ]
            return jnp.concatenate(parts, axis=1)

        field = jnp.concatenate(
            [line(-1)[ROWS - 2 :] * has_north, line(0), line(1)[0:2] * has_south], axis=0
        )
        taps_of(all_e, c, field)

    wo_flip = jnp.concatenate([wof[2 - a] for a in range(3)], axis=0).astype(BF)
    for r in range(ROWS + 2):
        d2[r] = (dot(patches(all_e, r), wo_flip, 0, 0) * s2[r]).astype(BF)
    clear(d2, 1)

    def weight_grad(turned, adj, base):
        for a in range(3):
            for b in range(3):
                at = base + (a * 3 + b) * CH
                grads[at : at + CH, :] = dot(turned[b, :, a * 128 : a * 128 + ROWS * 128], adj)

    weight_grad(t1, d2[1 : 1 + ROWS, 16 : 16 + COLS, :].reshape(ROWS * COLS, CH), 9 * CH)

    @pl.loop(0, 4)
    def _(k):
        r = k * 4
        g = conv_rows(d2, w2f[...], r, 4, 1) * s1[pl.ds(r + 2, 4)].reshape(4 * WIDE, CH)
        d1[pl.ds(r, 4)] = g.reshape(4, WIDE, CH)[:, 16 : 16 + COLS].astype(BF)

    weight_grad(t0, d1[...].reshape(ROWS * COLS, CH), 0)


def run_kernel(*args):
    vmem = pl.BlockSpec(memory_space=pltpu.VMEM)
    smem = pl.BlockSpec(memory_space=pltpu.SMEM)
    specs = [vmem] * 16
    specs[6] = smem
    specs[12] = smem
    dma = pltpu.SemaphoreType.DMA
    return pl.pallas_call(
        kernel,
        out_shape=(
            jax.ShapeDtypeStruct((18 * CH + 96, CH), F32),
            jax.ShapeDtypeStruct((8, 128), F32),
        ),
        in_specs=specs,
        out_specs=(vmem, vmem),
        scratch_shapes=[
            pltpu.VMEM((ROWS + 6, WIDE, CH), BF),
            pltpu.VMEM((ROWS + 6, WIDE, CH), BF),
            pltpu.VMEM((ROWS + 4, WIDE, CH), BF),
            pltpu.VMEM((ROWS + 2, WIDE, CH), BF),
            pltpu.VMEM((ROWS + 4, WIDE, CH), F32),
            pltpu.VMEM((ROWS + 2, WIDE, CH), F32),
            pltpu.VMEM((3 * CH, 3 * CH), BF),
            pltpu.VMEM((3 * CH, 3 * CH), BF),
            pltpu.VMEM((3 * CH, 3 * CH), BF),
            pltpu.VMEM((3, ROWS, COLS), F32),
            pltpu.VMEM((2, 3, ROWS, COLS), F32),
            pltpu.VMEM((384, PIX), BF),
            pltpu.VMEM((8, PIX), F32),
            pltpu.VMEM((8, PIX), F32),
            pltpu.VMEM((96, VW), F32),
            pltpu.VMEM((VW, 9 * VW), BF),
            pltpu.VMEM((VW, 9 * VW), BF),
            pltpu.VMEM((32, PIX + 256), BF),
            pltpu.VMEM((3, VW, PIX + 256), BF),
            pltpu.VMEM((3, VW, PIX + 256), BF),
            pltpu.VMEM((VW, PIX), F32),
            pltpu.VMEM((72, PIX + 256), F32),
            pltpu.VMEM((3, 3, 8, 128), F32),
            pltpu.VMEM((3, 3, 24, 128), F32),
            pltpu.VMEM((3, ROWS, COLS), BF),
            pltpu.VMEM((8, 3, ROWS, COLS), BF),
            pltpu.VMEM((ROWS + 4, 32, 256), F32),
            pltpu.VMEM((ROWS + 4, 32, 256), F32),
            pltpu.VMEM((ROWS + 2, WIDE, CH), BF),
            pltpu.VMEM((ROWS, COLS, CH), BF),
            pltpu.VMEM((3, CH, (ROWS + 2) * COLS), BF),
            pltpu.VMEM((3, CH, (ROWS + 2) * COLS), BF),
            pltpu.VMEM((1, 512), F32),
            pltpu.VMEM((3, 32, CH), F32),
            dma((8,)), dma((8,)), dma((2,)), dma((2,)), dma((2,)), dma((2,)), dma((8,)), dma((8,)),
        ],
        compiler_params=pltpu.CompilerParams(
            collective_id=0, has_side_effects=True, vmem_limit_bytes=56 * 1024 * 1024
        ),
    )(*args)


def per_device(
    features,
    conv_one_w,
    conv_one_b,
    conv_two_w,
    conv_two_b,
    out_conv_w,
    out_conv_b,
    vgg_one_w,
    vgg_one_b,
    vgg_two_w,
    vgg_two_b,
    lin_weights,
    row_lists,
    tap_index,
    tap_weight,
    target_tiles,
):
    grads, loss = run_kernel(
        features,
        conv_one_w,
        conv_one_b.reshape(1, CH),
        conv_two_w,
        conv_two_b.reshape(1, CH),
        jnp.transpose(out_conv_w, (0, 1, 3, 2)),
        out_conv_b,
        jnp.transpose(vgg_one_w, (1, 2, 3, 0)),
        vgg_one_b.reshape(1, VW),
        jnp.transpose(vgg_two_w, (2, 3, 0, 1)),
        vgg_two_b.reshape(1, VW),
        lin_weights.reshape(1, VW),
        row_lists,
        tap_index[0],
        tap_weight[0],
        target_tiles[0],
    )
    loss, grads = lax.psum((loss[0, 0], grads), ("lon", "grp"))
    grad_one = grads[: 9 * CH].reshape(3, 3, CH, CH)
    grad_two = grads[9 * CH : 18 * CH].reshape(3, 3, CH, CH)
    grad_out = grads[18 * CH :].reshape(3, 4, 8, CH)[:, :3, :3]
    return loss, grad_one, grad_two, jnp.transpose(grad_out, (0, 1, 3, 2))


def solution(mesh):
    in_specs = (
        P("grp", "lon", None),
        P(),
        P(),
        P(),
        P(),
        P(),
        P(),
        P(),
        P(),
        P(),
        P(),
        P(),
        P(("lon", "grp"), None, None),
        P(("lon", "grp"), None, None),
        P(("lon", "grp"), None, None),
        P(("lon", "grp"), None, None, None),
    )
    out_specs = (P(), P(), P(), P())
    return jax.shard_map(
        per_device, mesh=mesh, in_specs=in_specs, out_specs=out_specs, check_vma=False
    )
```

time: 1100 us -> 241 us (0.22)
  local copies, waits for them, and re-layouts: 424 us -> 6.18 us
  other arithmetic: 230 us -> 0 us
  matrix products: 107 us -> 0 us
  waiting for transfers between devices: 166 us -> 79.5 us
  starting transfers between devices: 79.7 us -> 0.04 us
  Pallas kernels: 0 us -> 78.3 us
    gather x2 -> x0, local copies, waits for them, and re-layouts: 354 us -> none  [the longest x1 354 us: per_device(): values = received[block_index, :, column]]
    unnamed x6 -> x0, other arithmetic: 176 us -> none
    conv_general_dilated x11 -> x0, matrix products: 93.9 us -> none  [the longest x6 74.5 us: conv_same(): lax.conv_general_dilated(picture[None], weight, (1, 1), 'SAME', dimension...]
    ppermute x24 -> x0, waiting for transfers between devices: 83.7 us -> none  [the longest x10 60.5 us: extended(): lax.ppermute(tail, axis, [(i, (i + 1) % count) for i in range(ends)])]
    ppermute x24 -> x0, starting transfers between devices: 79.6 us -> none  [the longest x10 40.4 us: extended(): lax.ppermute(head, axis, [((i + 1) % count, i) for i in range(ends)])]
    pallas_call x0 -> x1, Pallas kernels: none -> 78.3 us  [run_kernel(): pl.pallas_call(kernel, out_shape=(jax.ShapeDtypeStruct((18 * CH + 96, CH)...]
    unnamed x135 -> x1, local copies, waits for them, and re-layouts: 30.8 us -> 1.26 us
    conv_general_dilated x35 -> x0, local copies, waits for them, and re-layouts: 21.1 us -> none  [the longest x10 12.2 us: conv_same(): lax.conv_general_dilated(picture[None], weight, (1, 1), 'SAME', dimension...]
  transfers between devices with their start and end apart: 25 -> 1, of which waited for: 14 -> 1; matrix products, arithmetic and copies ran while one was open for 2% -> 0% of each run, Pallas kernels for 0% -> 0%
where the time goes in v1:
time: 241 us
  waiting for transfers between devices  79.5 us (33%)
  Pallas kernels  78.3 us (32%)
  blocking collectives  62.9 us (26%)
  between operations  14 us (6%)
  local copies, waits for them, and re-layouts  6.18 us (3%)
    psum x1, waiting for transfers between devices, per_device(): loss, grads = lax.psum((loss[0, 0], grads), ('lon', 'grp'))  79.5 us
    pallas_call x1, Pallas kernels, run_kernel(): pl.pallas_call(kernel, out_shape=(jax.ShapeDtypeStruct((18 * CH + 96, CH)...  78.3 us
    psum x1, blocking collectives, per_device(): loss, grads = lax.psum((loss[0, 0], grads), ('lon', 'grp'))  62.9 us
  transfers between devices with their start and end apart: 1, of which 1 were waited for; matrix products, arithmetic and copies ran while one was open for 0% of the time, Pallas kernels for 0%

profile of v1, /device:TPU:1, one launch (start us, length us, event | category | flops | bytes accessed | tf_op | source)
XLA Modules:
  0.0 240.9 jit_solution(3943939773943890138)
XLA Ops:
  7.2 0.0 all-reduce.2.cloned.1.call-start
  7.2 1.3 copy.20.rows_ref
  8.5 78.3 %shard_map.183 = (f32[2400,128]{1,0:T(8,128)}, f32[8,128]{1,0:T(8,128)}) custom-call(bf16[16,128,128]{2,1,0:T(8,128)(2,1)} %feat.1, bf16[3,3,128,128]{3,2,1,0:T(8,128)(2,1)} %w1.1, f32[1,128]{1,0:T(1,128)} %bitcast.26, bf16[3,3,128,128]{3,2,1,0:T(8,128)(2,1)} %w2.1, f32[1,128]{1,0:T(1,128)} %bitcast.27, bf16[3,3,3,128]{3,2,1,0:T(4,128)(2,1)} %bitcast.24, ...), custom_call_target="tpu_custom_call" | custom-call | tf_op jit(solution)/shard_map/pallas_call | solution.py:501
  86.8 0.0 all-reduce.2.cloned.1.call-update
  86.8 1.2 slice.15
  88.0 62.9 %psum.14 = f32[]{:T(128)} all-reduce(f32[]{:T(128)} %bitcast.11), channel_id=1, replica_groups=mesh['lon'=32,'grp'=4] {'lon','grp'}, use_global_device_ids=true, to_apply=%region_0.0 | all-reduce | flops 1 | bytes 8 | tf_op jit(solution)/shard_map/psum | solution.py:588
  150.8 79.5 %all-reduce.2.cloned.1.call-done = f32[2400,128]{1,0:T(8,128)} async-done(((f32[2400,128]{1,0:T(8,128)}), f32[2400,128]{1,0:T(8,128)}) %all-reduce.2.cloned.1.call-update) | async-done | bytes 1228816 | tf_op jit(solution)/shard_map/psum | solution.py:588
  230.3 0.8 slice.22
  231.1 0.6 slice_bitcast_fusion
  231.7 2.3 fusion
Async XLA Ops:
  7.2 223.1 %all-reduce.2.cloned.1.call-start = ((), (), s32[]{:S(2)}) async-start(), calls=%async_computation | async-start | bytes 2457600 | tf_op jit(solution)/shard_map/psum | solution.py:588
Sparse Core Ops, SparseCore 0:
  86.9 143.3 all-reduce.1

commit v2 on v1

--- a/solution.py
+++ b/solution.py
@@ -21,6 +21,110 @@
 MESH = pl.DeviceIdType.MESH
 
 AROUND = ((-1, -1), (-1, 0), (-1, 1), (0, -1), (0, 1), (1, -1), (1, 0), (1, 1))
+
+
+PARTS = ((0, (1, 2)), (1, (0, 2)), (2, (0, 1)))
+GRAD_ROWS = 2496
+PART = GRAD_ROWS // 3
+SHARE = PART // 8
+LINE_STEPS = [(d, k) for d in range(4) for k in range(2) if (d, k) != (0, 0)]
+PLANE_STEPS = [(d, e) for d in range(4) for e in range(4) if (d, e) != (0, 0)]
+
+
+def place():
+    lon, grp = lax.axis_index("lon"), lax.axis_index("grp")
+    return (lon // 8, (lon % 2) * 2 + grp // 2, (lon // 2) % 4), grp % 2
+
+
+def device(xyz, core):
+    x, y, z = xyz
+    return ((x * 4 + z) * 2 + y // 2, (y % 2) * 2 + core)
+
+
+def line_peers(axis):
+    xyz, core = place()
+    for d, k in LINE_STEPS:
+        at, its_core = (xyz[axis] + d) % 4, (core + k) % 2
+        peer = tuple(at if i == axis else xyz[i] for i in range(3))
+        yield device(peer, its_core), at * 2 + its_core
+
+
+def plane_peers(axes):
+    xyz, core = place()
+    u, v = axes
+    for d, e in PLANE_STEPS:
+        at_u, at_v = (xyz[u] + d) % 4, (xyz[v] + e) % 4
+        peer = tuple(at_u if i == u else at_v if i == v else xyz[i] for i in range(3))
+        yield device(peer, core), at_u * 4 + at_v
+
+
+def sum_offsets():
+    found = set()
+    for axis, axes in PARTS:
+        for d, k in LINE_STEPS:
+            found.add(tuple(d if i == axis else 0 for i in range(3)) + (k,))
+        for d, e in PLANE_STEPS:
+            found.add(tuple(d if i == axes[0] else e if i == axes[1] else 0 for i in range(3)) + (0,))
+    return sorted(found)
+
+
+def rows8(start, size):
+    return pl.ds(pl.multiple_of(start, 8), size)
+
+
+def send(src, dst, send_sem, recv_sem, to):
+    copy = pltpu.make_async_remote_copy(
+        src_ref=src, dst_ref=dst, send_sem=send_sem, recv_sem=recv_sem, device_id=to, device_id_type=MESH
+    )
+    copy.start()
+    return copy
+
+
+def sum_all(grads, out, line_in, line_sum, plane_in, plane_sum, gathered, sems):
+    ls, lr, ps, pr, gs, gr, os, orr = sems
+    xyz, core = place()
+    sent = []
+    first = []
+    for p, (axis, axes) in enumerate(PARTS):
+        for i, (peer, index) in enumerate(line_peers(axis)):
+            src = grads.at[rows8(p * PART + index * SHARE, SHARE)]
+            first.append(send(src, line_in.at[p, i], ls.at[p, i], lr.at[p, i], peer))
+    second = []
+    for p, (axis, axes) in enumerate(PARTS):
+        mine = xyz[axis] * 2 + core
+        for copy in first[p * 7 : p * 7 + 7]:
+            copy.wait()
+        total = grads[rows8(p * PART + mine * SHARE, SHARE), :]
+        for i in range(7):
+            total = total + line_in[p, i]
+        line_sum[p, 0:SHARE] = total
+        for i, (peer, index) in enumerate(plane_peers(axes)):
+            src = line_sum.at[p, rows8(index * 8, 8)]
+            second.append(send(src, plane_in.at[p, i], ps.at[p, i], pr.at[p, i], peer))
+    third = []
+    for p, (axis, axes) in enumerate(PARTS):
+        mine = xyz[axes[0]] * 4 + xyz[axes[1]]
+        for copy in second[p * 15 : p * 15 + 15]:
+            copy.wait()
+        total = line_sum[p, rows8(mine * 8, 8), :]
+        for i in range(15):
+            total = total + plane_in[p, i]
+        plane_sum[p] = total
+        gathered[p, rows8(mine * 8, 8), :] = total
+        for i, (peer, index) in enumerate(plane_peers(axes)):
+            dst = gathered.at[p, rows8(mine * 8, 8)]
+            third.append(send(plane_sum.at[p], dst, gs.at[p, i], gr.at[p, i], peer))
+    fourth = []
+    for p, (axis, axes) in enumerate(PARTS):
+        mine = xyz[axis] * 2 + core
+        at = rows8(p * PART + mine * SHARE, SHARE)
+        for copy in third[p * 15 : p * 15 + 15]:
+            copy.wait()
+        for i, (peer, index) in enumerate(line_peers(axis)):
+            fourth.append(send(gathered.at[p, 0:SHARE], out.at[at], os.at[p, i], orr.at[p, i], peer))
+        out[at, :] = gathered[p, 0:SHARE]
+    for copy in fourth:
+        copy.wait()
 
 
 def dot(a, b, ca=1, cb=0):
@@ -118,10 +222,12 @@
 
 def kernel(
     feat, w1, b1, w2, b2, wo, bo, v1w, v1b, v2w, v2b, lin, rows_ref, tap_i, tap_w, target,
-    grads, loss_out,
+    one_out, two_out, rest_out,
     f_ref, a0, a1, a2, s1, s2, w1c, w2c, w2f, c_own, c_near, hot, al, ar, v1f, v2c, v2t,
     zs, fs, gs, unit_t, y_ref, tb, pb, ca, ca_near, own_e, all_e, d2, d1, t0, t1, loss_acc, wof,
-    halo_send, halo_recv, col_send, col_recv, tab_send, tab_recv, adj_send, adj_recv,
+    grads, total, line_in, line_sum, plane_in, plane_sum, gathered,
+    halo_send, halo_recv, col_send, col_recv, tab_send, tab_recv, adj_send, adj_recv, out_sem,
+    *sum_sems,
 ):
     lon, grp = lax.axis_index("lon"), lax.axis_index("grp")
     n_lon, n_grp = lax.axis_size("lon"), lax.axis_size("grp")
@@ -132,6 +238,11 @@
     barrier = pltpu.get_barrier_semaphore()
     for dl, dg in AROUND:
         pl.semaphore_signal(barrier, inc=1, device_id=near(dl, dg), device_id_type=MESH)
+    xyz, core = place()
+    peers = sum_offsets()
+    for off in peers:
+        peer = device([(xyz[i] + off[i]) % 4 for i in range(3)], (core + off[3]) % 2)
+        pl.semaphore_signal(barrier, inc=1, device_id=peer, device_id_type=MESH)
 
     for a in range(3):
         for b in range(3):
@@ -167,7 +278,7 @@
     own_e[...] = jnp.zeros_like(own_e)
     all_e[...] = jnp.zeros_like(all_e)
 
-    pl.semaphore_wait(barrier, len(AROUND))
+    pl.semaphore_wait(barrier, len(AROUND) + len(peers))
     take_r = {-1: pl.ds(0, 3), 0: pl.ds(0, ROWS), 1: pl.ds(ROWS - 3, 3)}
     take_c = {-1: pl.ds(0, 16), 0: pl.ds(0, COLS), 1: pl.ds(COLS - 16, 16)}
     land_r = {-1: pl.ds(ROWS + 3, 3), 0: pl.ds(3, ROWS), 1: pl.ds(0, 3)}
@@ -300,7 +411,7 @@
     for copy in colours:
         copy.wait()
 
-    start = rows_ref[0, 1, 0]
+    start = rows_ref[1, 0, 0]
     slabs = (c_near.at[0], c_own, c_near.at[1])
     table = jnp.concatenate(
         [
@@ -347,7 +458,10 @@
         shift_store(gs, jnp.where(f > 0.0, g, 0.0), k * 4, 4)
 
     loss = jnp.sum(loss_acc[...], axis=1, keepdims=True) * (1.0 / PIX)
-    loss_out[...] = jnp.broadcast_to(loss, (8, 128))
+    grads[18 * CH + 96 : 18 * CH + 104, :] = jnp.broadcast_to(loss, (8, 128))
+    grads[18 * CH + 104 :, :] = jnp.zeros((GRAD_ROWS - 18 * CH - 104, CH), F32)
+    for p in range(3):
+        line_sum[p, SHARE:] = jnp.zeros((128 - SHARE, CH), F32)
 
     v1_back = jnp.concatenate(
         [
@@ -413,7 +527,7 @@
         copy.wait()
 
     for c in range(3):
-        placed = sum(pb[k, c, pl.ds(8 - rows_ref[0, k, 0], ROWS), :] for k in range(3))
+        placed = sum(pb[k, c, pl.ds(8 - rows_ref[k, 0, 0], ROWS), :] for k in range(3))
         ca[c] = placed.astype(BF)
 
     exchanged = []
@@ -490,6 +604,17 @@
 
     weight_grad(t0, d1[...].reshape(ROWS * COLS, CH), 0)
 
+    sum_all(grads, total, line_in, line_sum, plane_in, plane_sum, gathered, sum_sems)
+    outs = []
+    for i, (out, at, size) in enumerate(
+        ((one_out, 0, 9 * CH), (two_out, 9 * CH, 9 * CH), (rest_out, 18 * CH, 104))
+    ):
+        copy = pltpu.make_async_copy(total.at[at : at + size], out, out_sem.at[i])
+        copy.start()
+        outs.append(copy)
+    for copy in outs:
+        copy.wait()
+
 
 def run_kernel(*args):
     vmem = pl.BlockSpec(memory_space=pltpu.VMEM)
@@ -501,11 +626,12 @@
     return pl.pallas_call(
         kernel,
         out_shape=(
-            jax.ShapeDtypeStruct((18 * CH + 96, CH), F32),
-            jax.ShapeDtypeStruct((8, 128), F32),
+            jax.ShapeDtypeStruct((9 * CH, CH), F32),
+            jax.ShapeDtypeStruct((9 * CH, CH), F32),
+            jax.ShapeDtypeStruct((104, CH), F32),
         ),
         in_specs=specs,
-        out_specs=(vmem, vmem),
+        out_specs=(pl.BlockSpec(memory_space=pl.ANY),) * 3,
         scratch_shapes=[
             pltpu.VMEM((ROWS + 6, WIDE, CH), BF),
             pltpu.VMEM((ROWS + 6, WIDE, CH), BF),
@@ -541,7 +667,16 @@
             pltpu.VMEM((3, CH, (ROWS + 2) * COLS), BF),
             pltpu.VMEM((1, 512), F32),
             pltpu.VMEM((3, 32, CH), F32),
-            dma((8,)), dma((8,)), dma((2,)), dma((2,)), dma((2,)), dma((2,)), dma((8,)), dma((8,)),
+            pltpu.VMEM((GRAD_ROWS, CH), F32),
+            pltpu.VMEM((GRAD_ROWS, CH), F32),
+            pltpu.VMEM((3, 7, SHARE, CH), F32),
+            pltpu.VMEM((3, 128, CH), F32),
+            pltpu.VMEM((3, 15, 8, CH), F32),
+            pltpu.VMEM((3, 8, CH), F32),
+            pltpu.VMEM((3, 128, CH), F32),
+            dma((8,)), dma((8,)), dma((2,)), dma((2,)), dma((2,)), dma((2,)), dma((8,)), dma((8,)), dma((3,)),
+            dma((3, 7)), dma((3, 7)), dma((3, 15)), dma((3, 15)),
+            dma((3, 15)), dma((3, 15)), dma((3, 7)), dma((3, 7)),
         ],
         compiler_params=pltpu.CompilerParams(
             collective_id=0, has_side_effects=True, vmem_limit_bytes=56 * 1024 * 1024
@@ -567,7 +702,7 @@
     tap_weight,
     target_tiles,
 ):
-    grads, loss = run_kernel(
+    grad_one, grad_two, rest = run_kernel(
         features,
         conv_one_w,
         conv_one_b.reshape(1, CH),
@@ -580,16 +715,18 @@
         jnp.transpose(vgg_two_w, (2, 3, 0, 1)),
         vgg_two_b.reshape(1, VW),
         lin_weights.reshape(1, VW),
-        row_lists,
+        jnp.transpose(row_lists, (1, 0, 2)),
         tap_index[0],
         tap_weight[0],
         target_tiles[0],
     )
-    loss, grads = lax.psum((loss[0, 0], grads), ("lon", "grp"))
-    grad_one = grads[: 9 * CH].reshape(3, 3, CH, CH)
-    grad_two = grads[9 * CH : 18 * CH].reshape(3, 3, CH, CH)
-    grad_out = grads[18 * CH :].reshape(3, 4, 8, CH)[:, :3, :3]
-    return loss, grad_one, grad_two, jnp.transpose(grad_out, (0, 1, 3, 2))
+    grad_out = rest[:96].reshape(3, 4, 8, CH)[:, :3, :3]
+    return (
+        rest[96, 0],
+        grad_one.reshape(3, 3, CH, CH),
+        grad_two.reshape(3, 3, CH, CH),
+        jnp.transpose(grad_out, (0, 1, 3, 2)),
+    )
 
 
 def solution(mesh):

time: 241 us -> 110 us (0.46)
  waiting for transfers between devices: 79.5 us -> 0 us
  blocking collectives: 62.9 us -> 0 us
  Pallas kernels: 78.3 us -> 104 us
  between operations: 14 us -> 0.65 us
    psum x1 -> x0, waiting for transfers between devices: 79.5 us -> none  [per_device(): loss, grads = lax.psum((loss[0, 0], grads), ('lon', 'grp'))]
    psum x1 -> x0, blocking collectives: 62.9 us -> none  [per_device(): loss, grads = lax.psum((loss[0, 0], grads), ('lon', 'grp'))]
    pallas_call x1, Pallas kernels: 78.3 us -> 104 us  [run_kernel(): pl.pallas_call(kernel, out_shape=(jax.ShapeDtypeStruct((9 * CH, CH), F32)...]
  transfers between devices with their start and end apart: 1 -> 0, of which waited for: 1 -> 0; matrix products, arithmetic and copies ran while one was open for 0% -> 0% of each run, Pallas kernels for 0% -> 0%
where the time goes in v2:
time: 110 us
  Pallas kernels  104 us (95%)
  local copies, waits for them, and re-layouts  5.39 us (5%)
    pallas_call x1, Pallas kernels, run_kernel(): pl.pallas_call(kernel, out_shape=(jax.ShapeDtypeStruct((9 * CH, CH), F32)...  104 us
    unnamed x4, local copies, waits for them, and re-layouts  2.8 us

profile of v2, /device:TPU:1, one launch (start us, length us, event | category | flops | bytes accessed | tf_op | source)
XLA Modules:
  0.0 110.1 jit_solution(11058212841853728922)
XLA Ops:
  0.6 104.0 %shard_map.183 = (f32[1152,128]{1,0:T(8,128)}, f32[1152,128]{1,0:T(8,128)}, f32[104,128]{1,0:T(8,128)}) custom-call(bf16[16,128,128]{2,1,0:T(8,128)(2,1)} %feat.1, bf16[3,3,128,128]{3,2,1,0:T(8,128)(2,1)} %w1.1, f32[1,128]{1,0:T(1,128)} %bitcast.28, bf16[3,3,128,128]{3,2,1,0:T(8,128)(2,1)} %w2.1, f32[1,128]{1,0:T(1,128)} %bitcast.29, ...), custom_call_target="tpu_custom_call" | custom-call | tf_op jit(solution)/shard_map/pallas_call | solution.py:626
  104.7 0.8 slice.10
  105.5 0.6 slice_bitcast_fusion
  106.1 1.2 %slice.9 = f32[1,1]{1,0:T(1,128)} slice(f32[104,128]{1,0:T(8,128)} %get-tuple-element.7), slice={[96:97], [0:1]} | slice | bytes 8 | tf_op jit(solution)/shard_map/slice | solution.py:725
  107.3 0.0 copy-start
  107.3 2.0 %copy.22 = f32[3,3,128,128]{3,2,1,0:T(8,128)} copy(f32[3,3,128,128]{3,2,1,0:T(8,128)} %bitcast.19) | data formatting | bytes 1179648
  109.2 0.0 copy-done
  109.2 0.8 copy.23
Async XLA Ops:
  107.3 2.0 %copy-start = (f32[1152,128]{1,0:T(8,128)S(1)}, f32[1152,128]{1,0:T(8,128)}, u32[]{:S(2)}) copy-start(f32[1152,128]{1,0:T(8,128)} %get-tuple-element.9) | copy-start | bytes 1769476

commit v3 on v2

--- a/solution.py
+++ b/solution.py
@@ -25,6 +25,8 @@
 
 PARTS = ((0, (1, 2)), (1, (0, 2)), (2, (0, 1)))
 GRAD_ROWS = 2496
+REST = 9 * CH
+ONE = 9 * CH + 104
 PART = GRAD_ROWS // 3
 SHARE = PART // 8
 LINE_STEPS = [(d, k) for d in range(4) for k in range(2) if (d, k) != (0, 0)]
@@ -80,15 +82,17 @@
     return copy
 
 
-def sum_all(grads, out, line_in, line_sum, plane_in, plane_sum, gathered, sems):
+def scatter_part(p, grads, line_in, sems):
+    copies = []
+    for i, (peer, index) in enumerate(line_peers(PARTS[p][0])):
+        src = grads.at[rows8(p * PART + index * SHARE, SHARE)]
+        copies.append(send(src, line_in.at[p, i], sems[0].at[p, i], sems[1].at[p, i], peer))
+    return copies
+
+
+def sum_all(first, grads, out, line_in, line_sum, plane_in, plane_sum, gathered, sems):
     ls, lr, ps, pr, gs, gr, os, orr = sems
     xyz, core = place()
-    sent = []
-    first = []
-    for p, (axis, axes) in enumerate(PARTS):
-        for i, (peer, index) in enumerate(line_peers(axis)):
-            src = grads.at[rows8(p * PART + index * SHARE, SHARE)]
-            first.append(send(src, line_in.at[p, i], ls.at[p, i], lr.at[p, i], peer))
     second = []
     for p, (axis, axes) in enumerate(PARTS):
         mine = xyz[axis] * 2 + core
@@ -200,7 +204,7 @@
 
 
 def vgg_first(zs, fs, v1, v1b, n):
-    @pl.loop(0, TROWS // n)
+    @pl.loop(0, TROWS // n, unroll=4)
     def _(k):
         r0 = k * n
         rhs = jnp.concatenate(
@@ -243,6 +247,25 @@
     for off in peers:
         peer = device([(xyz[i] + off[i]) % 4 for i in range(3)], (core + off[3]) % 2)
         pl.semaphore_signal(barrier, inc=1, device_id=peer, device_id_type=MESH)
+
+    pl.semaphore_wait(barrier, len(AROUND) + len(peers))
+    take_r = {-1: pl.ds(0, 3), 0: pl.ds(0, ROWS), 1: pl.ds(ROWS - 3, 3)}
+    take_c = {-1: pl.ds(0, 16), 0: pl.ds(0, COLS), 1: pl.ds(COLS - 16, 16)}
+    land_r = {-1: pl.ds(ROWS + 3, 3), 0: pl.ds(3, ROWS), 1: pl.ds(0, 3)}
+    land_c = {-1: pl.ds(COLS + 16, 16), 0: pl.ds(16, COLS), 1: pl.ds(0, 16)}
+    halo = []
+    for i, (dl, dg) in enumerate(AROUND):
+        copy = pltpu.make_async_remote_copy(
+            src_ref=feat.at[take_r[dg], take_c[dl]],
+            dst_ref=f_ref.at[land_r[dg], land_c[dl]],
+            send_sem=halo_send.at[i],
+            recv_sem=halo_recv.at[i],
+            device_id=near(dl, dg),
+            device_id_type=MESH,
+        )
+        copy.start()
+        halo.append(copy)
+    f_ref[3 : 3 + ROWS, 16 : 16 + COLS, :] = feat[...]
 
     for a in range(3):
         for b in range(3):
@@ -278,43 +301,19 @@
     own_e[...] = jnp.zeros_like(own_e)
     all_e[...] = jnp.zeros_like(all_e)
 
-    pl.semaphore_wait(barrier, len(AROUND) + len(peers))
-    take_r = {-1: pl.ds(0, 3), 0: pl.ds(0, ROWS), 1: pl.ds(ROWS - 3, 3)}
-    take_c = {-1: pl.ds(0, 16), 0: pl.ds(0, COLS), 1: pl.ds(COLS - 16, 16)}
-    land_r = {-1: pl.ds(ROWS + 3, 3), 0: pl.ds(3, ROWS), 1: pl.ds(0, 3)}
-    land_c = {-1: pl.ds(COLS + 16, 16), 0: pl.ds(16, COLS), 1: pl.ds(0, 16)}
-    halo = []
-    for i, (dl, dg) in enumerate(AROUND):
-        copy = pltpu.make_async_remote_copy(
-            src_ref=feat.at[take_r[dg], take_c[dl]],
-            dst_ref=f_ref.at[land_r[dg], land_c[dl]],
-            send_sem=halo_send.at[i],
-            recv_sem=halo_recv.at[i],
-            device_id=near(dl, dg),
-            device_id_type=MESH,
-        )
-        copy.start()
-        halo.append(copy)
-    f_ref[3 : 3 + ROWS, 16 : 16 + COLS, :] = feat[...]
-
     for r in range(TROWS):
         tgt = target[:, r, :].astype(F32)
         unit_t[0:8, r * 128 : (r + 1) * 128] = jnp.concatenate(
             [tgt, jnp.zeros((5, 128), F32)], axis=0
         )
 
-    @pl.loop(0, 8)
+    @pl.loop(0, 8, unroll=4)
     def _(k):
         store_scaled(zs, unit_t[0:8, span(k * 1024, 1024, 128)], k * 8, 8)
 
     vgg_first(zs, fs, v1, v1b_col, 4)
 
-    @pl.loop(0, TROWS // 4)
-    def _(k):
-        f = jnp.maximum(dot(v2c[...], nine_taps(fs, k * 4, 4)) + v2b_col, 0.0)
-        unit_t[:, span(k * 512, 512, 128)] = f * inv_norm(f)
-
-    @pl.loop(0, 8)
+    @pl.loop(0, 8, unroll=4)
     def _(k):
         at = span(k * 1024, 1024, 128)
         index = tap_i[:, at]
@@ -342,7 +341,7 @@
         copy.wait()
     north, south = grp == 0, grp == n_grp - 1
 
-    @pl.loop(0, ROWS + 6)
+    @pl.loop(0, ROWS + 6, unroll=2)
     def _(r):
         a0[r] = act_slope(f_ref[r])[0]
 
@@ -357,7 +356,7 @@
 
     clear(a0, 3)
 
-    @pl.loop(0, 5)
+    @pl.loop(0, 5, unroll=5)
     def _(k):
         r = k * 4
         h = (conv_rows(a0, w1c[...], r, 4) + b1[...]).astype(BF)
@@ -367,7 +366,7 @@
 
     clear(a1, 2)
 
-    @pl.loop(0, 6)
+    @pl.loop(0, 6, unroll=3)
     def _(k):
         r = k * 3
         f = f_ref[pl.ds(r + 2, 3)].reshape(3 * WIDE, CH).astype(F32)
@@ -399,14 +398,10 @@
         copy.start()
         colours.append(copy)
 
-    for act, turned, first_row in ((a0, t0, 2), (a1, t1, 1)):
-
-        @pl.loop(0, ROWS + 2)
-        def _(r, act=act, turned=turned, first_row=first_row):
-            block = act[r + first_row].astype(F32).T
-            at = span(r * 128, 128, 128)
-            for b in range(3):
-                turned[b, :, at] = block[:, 15 + b : 15 + b + COLS].astype(BF)
+    @pl.loop(0, TROWS // 4, unroll=4)
+    def _(k):
+        f = jnp.maximum(dot(v2c[...], nine_taps(fs, k * 4, 4)) + v2b_col, 0.0)
+        unit_t[:, span(k * 512, 512, 128)] = f * inv_norm(f)
 
     for copy in colours:
         copy.wait()
@@ -425,7 +420,7 @@
     table_lo = (table - table_hi.astype(F32)).astype(BF)
     table = jnp.concatenate([table_hi, table_lo], axis=0)
 
-    @pl.loop(0, 8)
+    @pl.loop(0, 8, unroll=4)
     def _(k):
         at = span(k * 1024, 1024, 128)
         got = dot(table, hot[:, at])
@@ -445,7 +440,7 @@
     vgg_first(zs, fs, v1, v1b_col, 4)
     loss_acc[...] = jnp.zeros_like(loss_acc)
 
-    @pl.loop(0, TROWS // 4)
+    @pl.loop(0, TROWS // 4, unroll=4)
     def _(k):
         f = jnp.maximum(dot(v2c[...], nine_taps(fs, k * 4, 4)) + v2b_col, 0.0)
         inv = inv_norm(f)
@@ -458,7 +453,7 @@
         shift_store(gs, jnp.where(f > 0.0, g, 0.0), k * 4, 4)
 
     loss = jnp.sum(loss_acc[...], axis=1, keepdims=True) * (1.0 / PIX)
-    grads[18 * CH + 96 : 18 * CH + 104, :] = jnp.broadcast_to(loss, (8, 128))
+    grads[REST + 96 : REST + 104, :] = jnp.broadcast_to(loss, (8, 128))
     grads[18 * CH + 104 :, :] = jnp.zeros((GRAD_ROWS - 18 * CH - 104, CH), F32)
     for p in range(3):
         line_sum[p, SHARE:] = jnp.zeros((128 - SHARE, CH), F32)
@@ -472,7 +467,7 @@
         axis=0,
     ).astype(BF)
 
-    @pl.loop(0, TROWS // 4)
+    @pl.loop(0, TROWS // 4, unroll=4)
     def _(k):
         g = dot(v2t[...], nine_taps(gs, k * 4, 4)).astype(BF)
         at = span((k * 4 + 1) * 128, 512, 128)
@@ -503,7 +498,7 @@
         lo = (spread - hi.astype(F32)).astype(BF)
         return acc + dot(jnp.concatenate([hi, lo], axis=0), hot[:, at], 1, 1)
 
-    acc = lax.fori_loop(0, 8, table_adjoint, jnp.zeros((96, 384), F32))
+    acc = lax.fori_loop(0, 8, table_adjoint, jnp.zeros((96, 384), F32), unroll=4)
     acc = acc[0:48] + acc[48:96]
     adjoint = acc[0:24] + pltpu.roll(acc[24:48], 1, 1)
     for k in range(3):
@@ -523,6 +518,15 @@
         )
         copy.start()
         returned.append(copy)
+    def turn(act, turned, first_row):
+        @pl.loop(0, ROWS + 2, unroll=3)
+        def _(r):
+            block = act[r + first_row].astype(F32).T
+            at = span(r * 128, 128, 128)
+            for b in range(3):
+                turned[b, :, at] = block[:, 15 + b : 15 + b + COLS].astype(BF)
+
+    turn(a1, t1, 1)
     for copy in returned:
         copy.wait()
 
@@ -561,9 +565,10 @@
     for r in range(ROWS + 2):
         grad_out += dot(patches(own_e, r), a2[r])
     for a in range(3):
-        base = 18 * CH + (2 - a) * 32
+        base = REST + (2 - a) * 32
         grads[base : base + 32, :] = grad_out[a * 32 : a * 32 + 32]
 
+    turn(a0, t0, 2)
     for copy in exchanged:
         copy.wait()
     at_of = {delta: i for i, delta in enumerate(AROUND)}
@@ -588,26 +593,31 @@
         d2[r] = (dot(patches(all_e, r), wo_flip, 0, 0) * s2[r]).astype(BF)
     clear(d2, 1)
 
-    def weight_grad(turned, adj, base):
-        for a in range(3):
-            for b in range(3):
-                at = base + (a * 3 + b) * CH
-                grads[at : at + CH, :] = dot(turned[b, :, a * 128 : a * 128 + ROWS * 128], adj)
-
-    weight_grad(t1, d2[1 : 1 + ROWS, 16 : 16 + COLS, :].reshape(ROWS * COLS, CH), 9 * CH)
-
-    @pl.loop(0, 4)
+    def weight_grad(turned, adj, base, taps):
+        for tap in taps:
+            a, b = tap // 3, tap % 3
+            at = base + tap * CH
+            grads[at : at + CH, :] = dot(turned[b, :, a * 128 : a * 128 + ROWS * 128], adj)
+
+    weight_grad(t1, d2[1 : 1 + ROWS, 16 : 16 + COLS, :].reshape(ROWS * COLS, CH), 0, range(9))
+    first = scatter_part(0, grads, line_in, sum_sems)
+
+    @pl.loop(0, 4, unroll=4)
     def _(k):
         r = k * 4
         g = conv_rows(d2, w2f[...], r, 4, 1) * s1[pl.ds(r + 2, 4)].reshape(4 * WIDE, CH)
         d1[pl.ds(r, 4)] = g.reshape(4, WIDE, CH)[:, 16 : 16 + COLS].astype(BF)
 
-    weight_grad(t0, d1[...].reshape(ROWS * COLS, CH), 0)
-
-    sum_all(grads, total, line_in, line_sum, plane_in, plane_sum, gathered, sum_sems)
+    d1_all = d1[...].reshape(ROWS * COLS, CH)
+    weight_grad(t0, d1_all, ONE, range(0, 4))
+    first += scatter_part(1, grads, line_in, sum_sems)
+    weight_grad(t0, d1_all, ONE, range(4, 9))
+    first += scatter_part(2, grads, line_in, sum_sems)
+
+    sum_all(first, grads, total, line_in, line_sum, plane_in, plane_sum, gathered, sum_sems)
     outs = []
     for i, (out, at, size) in enumerate(
-        ((one_out, 0, 9 * CH), (two_out, 9 * CH, 9 * CH), (rest_out, 18 * CH, 104))
+        ((one_out, ONE, 9 * CH), (two_out, 0, 9 * CH), (rest_out, REST, 104))
     ):
         copy = pltpu.make_async_copy(total.at[at : at + size], out, out_sem.at[i])
         copy.start()
@@ -684,6 +694,37 @@
     )(*args)
 
 
+def hand_over_kernel(one, two, rest, loss, one_out, two_out, grad_out, sems):
+    copies = []
+    for i, (src, dst) in enumerate(((one, one_out), (two, two_out))):
+        copy = pltpu.make_async_copy(src, dst, sems.at[i])
+        copy.start()
+        copies.append(copy)
+    for a in range(3):
+        for b in range(3):
+            grad_out[a, b] = rest[a * 32 + b * 8 : a * 32 + b * 8 + 3, :]
+    loss[...] = rest[96:97, 0:1]
+    for copy in copies:
+        copy.wait()
+
+
+def hand_over(one, two, rest):
+    vmem, hbm = pl.BlockSpec(memory_space=pltpu.VMEM), pl.BlockSpec(memory_space=pl.ANY)
+    block = jax.ShapeDtypeStruct((9 * CH, CH), F32)
+    return pl.pallas_call(
+        hand_over_kernel,
+        out_shape=(
+            jax.ShapeDtypeStruct((1, 1), F32),
+            block,
+            block,
+            jax.ShapeDtypeStruct((3, 3, 3, CH), F32),
+        ),
+        in_specs=[vmem, vmem, vmem],
+        out_specs=(vmem, hbm, hbm, vmem),
+        scratch_shapes=[pltpu.SemaphoreType.DMA((2,))],
+    )(one, two, rest)
+
+
 def per_device(
     features,
     conv_one_w,
@@ -720,9 +761,9 @@
         tap_weight[0],
         target_tiles[0],
     )
-    grad_out = rest[:96].reshape(3, 4, 8, CH)[:, :3, :3]
+    loss, grad_one, grad_two, grad_out = hand_over(grad_one, grad_two, rest)
     return (
-        rest[96, 0],
+        loss.reshape(()),
         grad_one.reshape(3, 3, CH, CH),
         grad_two.reshape(3, 3, CH, CH),
         jnp.transpose(grad_out, (0, 1, 3, 2)),

time: 110 us -> 91.2 us (0.83)
  Pallas kernels: 104 us -> 90.2 us
  local copies, waits for them, and re-layouts: 5.39 us -> 0 us
    pallas_call x1, Pallas kernels: 104 us -> 87.3 us  [run_kernel(): pl.pallas_call(kernel, out_shape=(jax.ShapeDtypeStruct((9 * CH, CH), F32)...]
    pallas_call x0 -> x1, Pallas kernels: none -> 2.88 us  [hand_over(): pl.pallas_call(hand_over_kernel, out_shape=(jax.ShapeDtypeStruct((1, 1),...]
    unnamed x4 -> x0, local copies, waits for them, and re-layouts: 2.8 us -> none
    slice x2 -> x0, local copies, waits for them, and re-layouts: 1.98 us -> none  [the longest x1 1.18 us: per_device(): rest[96, 0]]
where the time goes in v3:
time: 91.2 us; the launch traced here: 91 us
  Pallas kernels  90.2 us (99%)
    pallas_call x1, Pallas kernels, run_kernel(): pl.pallas_call(kernel, out_shape=(jax.ShapeDtypeStruct((9 * CH, CH), F32)...  87.3 us
    pallas_call x1, Pallas kernels, hand_over(): pl.pallas_call(hand_over_kernel, out_shape=(jax.ShapeDtypeStruct((1, 1),...  2.88 us

profile of v3, /device:TPU:1, one launch (start us, length us, event | category | flops | bytes accessed | tf_op | source)
XLA Modules:
  0.0 91.0 jit_solution(11596462442957630187)
XLA Ops:
  0.6 87.3 %shard_map.183 = (f32[1152,128]{1,0:T(8,128)}, f32[1152,128]{1,0:T(8,128)}, f32[104,128]{1,0:T(8,128)}) custom-call(bf16[16,128,128]{2,1,0:T(8,128)(2,1)} %feat.1, bf16[3,3,128,128]{3,2,1,0:T(8,128)(2,1)} %w1.1, f32[1,128]{1,0:T(1,128)} %bitcast.23, bf16[3,3,128,128]{3,2,1,0:T(8,128)(2,1)} %w2.1, f32[1,128]{1,0:T(1,128)} %bitcast.24, ...), custom_call_target="tpu_custom_call" | custom-call | tf_op jit(solution)/shard_map/pallas_call | solution.py:636
  88.0 2.9 %shard_map.184 = (f32[1,1]{1,0:T(1,128)}, f32[1152,128]{1,0:T(8,128)}, f32[1152,128]{1,0:T(8,128)}, f32[3,3,3,128]{3,2,1,0:T(4,128)}) custom-call(f32[1152,128]{1,0:T(8,128)} %get-tuple-element.11.one, f32[1152,128]{1,0:T(8,128)} %get-tuple-element.12.two, f32[104,128]{1,0:T(8,128)} %get-tuple-element.13.rest), custom_call_target="tpu_custom_call" | custom-call | tf_op jit(solution)/shard_map/pallas_call | solution.py:714

commit v4 on v3

--- a/solution.py
+++ b/solution.py
@@ -86,30 +86,32 @@
     copies = []
     for i, (peer, index) in enumerate(line_peers(PARTS[p][0])):
         src = grads.at[rows8(p * PART + index * SHARE, SHARE)]
-        copies.append(send(src, line_in.at[p, i], sems[0].at[p, i], sems[1].at[p, i], peer))
+        copies.append(send(src, line_in.at[p, i], sems[0].at[p], sems[1].at[p], peer))
     return copies
 
 
 def sum_all(first, grads, out, line_in, line_sum, plane_in, plane_sum, gathered, sems):
     ls, lr, ps, pr, gs, gr, os, orr = sems
+
+    def all_of(ref, sem):
+        pltpu.make_async_copy(ref, ref, sem).wait()
+
     xyz, core = place()
     second = []
     for p, (axis, axes) in enumerate(PARTS):
         mine = xyz[axis] * 2 + core
-        for copy in first[p * 7 : p * 7 + 7]:
-            copy.wait()
+        all_of(line_in.at[p], lr.at[p])
         total = grads[rows8(p * PART + mine * SHARE, SHARE), :]
         for i in range(7):
             total = total + line_in[p, i]
         line_sum[p, 0:SHARE] = total
         for i, (peer, index) in enumerate(plane_peers(axes)):
             src = line_sum.at[p, rows8(index * 8, 8)]
-            second.append(send(src, plane_in.at[p, i], ps.at[p, i], pr.at[p, i], peer))
+            second.append(send(src, plane_in.at[p, i], ps.at[p], pr.at[p], peer))
     third = []
     for p, (axis, axes) in enumerate(PARTS):
         mine = xyz[axes[0]] * 4 + xyz[axes[1]]
-        for copy in second[p * 15 : p * 15 + 15]:
-            copy.wait()
+        all_of(plane_in.at[p], pr.at[p])
         total = line_sum[p, rows8(mine * 8, 8), :]
         for i in range(15):
             total = total + plane_in[p, i]
@@ -117,18 +119,25 @@
         gathered[p, rows8(mine * 8, 8), :] = total
         for i, (peer, index) in enumerate(plane_peers(axes)):
             dst = gathered.at[p, rows8(mine * 8, 8)]
-            third.append(send(plane_sum.at[p], dst, gs.at[p, i], gr.at[p, i], peer))
+            third.append(send(plane_sum.at[p], dst, gs.at[p], gr.at[p], peer))
     fourth = []
     for p, (axis, axes) in enumerate(PARTS):
         mine = xyz[axis] * 2 + core
         at = rows8(p * PART + mine * SHARE, SHARE)
-        for copy in third[p * 15 : p * 15 + 15]:
-            copy.wait()
+        all_of(gathered.at[p, 0:120], gr.at[p])
         for i, (peer, index) in enumerate(line_peers(axis)):
-            fourth.append(send(gathered.at[p, 0:SHARE], out.at[at], os.at[p, i], orr.at[p, i], peer))
+            fourth.append(send(gathered.at[p, 0:SHARE], out.at[at], os.at[p], orr.at[p], peer))
         out[at, :] = gathered[p, 0:SHARE]
-    for copy in fourth:
-        copy.wait()
+    for p in range(3):
+        all_of(line_in.at[p], ls.at[p])
+        all_of(plane_in.at[p], ps.at[p])
+        all_of(gathered.at[p, 0:120], gs.at[p])
+    for p in range(3):
+        all_of(out.at[0 : 7 * SHARE], os.at[p])
+        all_of(out.at[0 : 7 * SHARE], orr.at[p])
+
+
+HALO_ORDER = (1, 6, 3, 4, 0, 2, 5, 7)
 
 
 def dot(a, b, ca=1, cb=0):
@@ -229,7 +238,7 @@
     one_out, two_out, rest_out,
     f_ref, a0, a1, a2, s1, s2, w1c, w2c, w2f, c_own, c_near, hot, al, ar, v1f, v2c, v2t,
     zs, fs, gs, unit_t, y_ref, tb, pb, ca, ca_near, own_e, all_e, d2, d1, t0, t1, loss_acc, wof,
-    grads, total, line_in, line_sum, plane_in, plane_sum, gathered,
+    side_out, side_in, grads, total, line_in, line_sum, plane_in, plane_sum, gathered,
     halo_send, halo_recv, col_send, col_recv, tab_send, tab_recv, adj_send, adj_recv, out_sem,
     *sum_sems,
 ):
@@ -248,23 +257,65 @@
         peer = device([(xyz[i] + off[i]) % 4 for i in range(3)], (core + off[3]) % 2)
         pl.semaphore_signal(barrier, inc=1, device_id=peer, device_id_type=MESH)
 
+    @pl.loop(0, 8, unroll=4)
+    def _(k):
+        at = span(k * 1024, 1024, 128)
+        index = tap_i[:, at]
+        weight = tap_w[:, at]
+        column = lax.shift_left(lax.shift_right_logical(index, 10), 7) + jnp.bitwise_and(index, 127)
+        slot = jnp.bitwise_and(lax.shift_right_logical(index, 7), 7)
+        left = jnp.min(column, axis=0, keepdims=True)
+        top = jnp.min(slot, axis=0, keepdims=True)
+        is_left, is_top = column == left, slot == top
+
+        def corner(cond):
+            return jnp.sum(jnp.where(cond, weight, 0.0), axis=0, keepdims=True)
+
+        not_left, not_top = jnp.logical_not(is_left), jnp.logical_not(is_top)
+        w_tl, w_tr = corner(is_top & is_left), corner(is_top & not_left)
+        w_bl, w_br = corner(not_top & is_left), corner(not_top & not_left)
+        j = lax.broadcasted_iota(jnp.int32, (8, 1024), 0)
+        on_top, on_next = j == top, j == top + 1
+        al[:, at] = jnp.where(on_top, w_tl, jnp.where(on_next, w_bl, 0.0))
+        ar[:, at] = jnp.where(on_top, w_tr, jnp.where(on_next, w_br, 0.0))
+        x = lax.broadcasted_iota(jnp.int32, (384, 1024), 0)
+        hot[:, at] = jnp.where(x == left, 1.0, 0.0).astype(BF)
+
+    side_out[0] = feat[:, 0:8, :].astype(F32).reshape(ROWS * 8, CH).astype(BF)
+    side_out[1] = feat[:, COLS - 8 :, :].astype(F32).reshape(ROWS * 8, CH).astype(BF)
     pl.semaphore_wait(barrier, len(AROUND) + len(peers))
-    take_r = {-1: pl.ds(0, 3), 0: pl.ds(0, ROWS), 1: pl.ds(ROWS - 3, 3)}
+    take_r = {-1: pl.ds(0, 3), 1: pl.ds(ROWS - 3, 3)}
     take_c = {-1: pl.ds(0, 16), 0: pl.ds(0, COLS), 1: pl.ds(COLS - 16, 16)}
-    land_r = {-1: pl.ds(ROWS + 3, 3), 0: pl.ds(3, ROWS), 1: pl.ds(0, 3)}
+    land_r = {-1: pl.ds(ROWS + 3, 3), 1: pl.ds(0, 3)}
     land_c = {-1: pl.ds(COLS + 16, 16), 0: pl.ds(16, COLS), 1: pl.ds(0, 16)}
+    north, south = grp == 0, grp == n_grp - 1
+    sends = {-1: grp > 0, 0: None, 1: grp < n_grp - 1}
+    lands = {-1: sends[1], 0: None, 1: sends[-1]}
+
+    def only_if(cond, act):
+        if cond is None:
+            act()
+        else:
+            pl.when(cond)(act)
+
     halo = []
-    for i, (dl, dg) in enumerate(AROUND):
+    for i in HALO_ORDER:
+        dl, dg = AROUND[i]
+        if dg == 0:
+            src, dst = side_out.at[(1 + dl) // 2], side_in.at[(1 + dl) // 2]
+        else:
+            src = feat.at[take_r[dg], take_c[dl]]
+            dst = f_ref.at[land_r[dg], land_c[dl]]
         copy = pltpu.make_async_remote_copy(
-            src_ref=feat.at[take_r[dg], take_c[dl]],
-            dst_ref=f_ref.at[land_r[dg], land_c[dl]],
+            src_ref=src,
+            dst_ref=dst,
             send_sem=halo_send.at[i],
             recv_sem=halo_recv.at[i],
             device_id=near(dl, dg),
             device_id_type=MESH,
         )
-        copy.start()
-        halo.append(copy)
+        only_if(sends[dg], copy.start)
+        halo.append((dg, copy))
     f_ref[3 : 3 + ROWS, 16 : 16 + COLS, :] = feat[...]
 
     for a in range(3):
@@ -313,37 +364,22 @@
 
     vgg_first(zs, fs, v1, v1b_col, 4)
 
-    @pl.loop(0, 8, unroll=4)
-    def _(k):
-        at = span(k * 1024, 1024, 128)
-        index = tap_i[:, at]
-        weight = tap_w[:, at]
-        column = lax.shift_left(lax.shift_right_logical(index, 10), 7) + jnp.bitwise_and(index, 127)
-        slot = jnp.bitwise_and(lax.shift_right_logical(index, 7), 7)
-        left = jnp.min(column, axis=0, keepdims=True)
-        top = jnp.min(slot, axis=0, keepdims=True)
-        is_left, is_top = column == left, slot == top
-
-        def corner(cond):
-            return jnp.sum(jnp.where(cond, weight, 0.0), axis=0, keepdims=True)
-
-        not_left, not_top = jnp.logical_not(is_left), jnp.logical_not(is_top)
-        w_tl, w_tr = corner(is_top & is_left), corner(is_top & not_left)
-        w_bl, w_br = corner(not_top & is_left), corner(not_top & not_left)
-        j = lax.broadcasted_iota(jnp.int32, (8, 1024), 0)
-        on_top, on_next = j == top, j == top + 1
-        al[:, at] = jnp.where(on_top, w_tl, jnp.where(on_next, w_bl, 0.0))
-        ar[:, at] = jnp.where(on_top, w_tr, jnp.where(on_next, w_br, 0.0))
-        x = lax.broadcasted_iota(jnp.int32, (384, 1024), 0)
-        hot[:, at] = jnp.where(x == left, 1.0, 0.0).astype(BF)
-
-    for copy in halo:
-        copy.wait()
-    north, south = grp == 0, grp == n_grp - 1
-
-    @pl.loop(0, ROWS + 6, unroll=2)
-    def _(r):
-        a0[r] = act_slope(f_ref[r])[0]
+    a0[3 : 3 + ROWS, 16 : 16 + COLS, :] = act_slope(feat[...])[0]
+    for dg, copy in halo:
+        only_if(sends[dg], copy.wait_send)
+        only_if(lands[dg], copy.wait_recv)
+    blank = jnp.zeros((ROWS, 8, CH), F32)
+    west = side_in[1].astype(F32).reshape(ROWS, 8, CH)
+    east = side_in[0].astype(F32).reshape(ROWS, 8, CH)
+    f_ref[3 : 3 + ROWS, 0:16, :] = jnp.concatenate([blank, west], axis=1).astype(BF)
+    f_ref[3 : 3 + ROWS, 16 + COLS :, :] = jnp.concatenate([east, blank], axis=1).astype(BF)
+    for rows, cols in (
+        (slice(0, 3), slice(0, WIDE)),
+        (slice(ROWS + 3, ROWS + 6), slice(0, WIDE)),
+        (slice(3, ROWS + 3), slice(0, 16)),
+        (slice(3, ROWS + 3), slice(16 + COLS, WIDE)),
+    ):
+        a0[rows, cols, :] = act_slope(f_ref[rows, cols, :])[0]
 
     def clear(ref, rows):
         @pl.when(north)
@@ -594,12 +630,12 @@
     clear(d2, 1)
 
     def weight_grad(turned, adj, base, taps):
-        for tap in taps:
-            a, b = tap // 3, tap % 3
-            at = base + tap * CH
-            grads[at : at + CH, :] = dot(turned[b, :, a * 128 : a * 128 + ROWS * 128], adj)
-
-    weight_grad(t1, d2[1 : 1 + ROWS, 16 : 16 + COLS, :].reshape(ROWS * COLS, CH), 0, range(9))
+        for a in taps:
+            at = base + a * 3 * CH
+            shifted = [turned[b, :, a * 128 : a * 128 + ROWS * 128] for b in range(3)]
+            grads[at : at + 3 * CH, :] = dot(jnp.concatenate(shifted, axis=0), adj)
+
+    weight_grad(t1, d2[1 : 1 + ROWS, 16 : 16 + COLS, :].reshape(ROWS * COLS, CH), 0, range(3))
     first = scatter_part(0, grads, line_in, sum_sems)
 
     @pl.loop(0, 4, unroll=4)
@@ -609,9 +645,9 @@
         d1[pl.ds(r, 4)] = g.reshape(4, WIDE, CH)[:, 16 : 16 + COLS].astype(BF)
 
     d1_all = d1[...].reshape(ROWS * COLS, CH)
-    weight_grad(t0, d1_all, ONE, range(0, 4))
+    weight_grad(t0, d1_all, ONE, range(0, 2))
     first += scatter_part(1, grads, line_in, sum_sems)
-    weight_grad(t0, d1_all, ONE, range(4, 9))
+    weight_grad(t0, d1_all, ONE, range(2, 3))
     first += scatter_part(2, grads, line_in, sum_sems)
 
     sum_all(first, grads, total, line_in, line_sum, plane_in, plane_sum, gathered, sum_sems)
@@ -677,6 +713,8 @@
             pltpu.VMEM((3, CH, (ROWS + 2) * COLS), BF),
             pltpu.VMEM((1, 512), F32),
             pltpu.VMEM((3, 32, CH), F32),
+            pltpu.VMEM((2, ROWS * 8, CH), BF),
+            pltpu.VMEM((2, ROWS * 8, CH), BF),
             pltpu.VMEM((GRAD_ROWS, CH), F32),
             pltpu.VMEM((GRAD_ROWS, CH), F32),
             pltpu.VMEM((3, 7, SHARE, CH), F32),
@@ -685,8 +723,7 @@
             pltpu.VMEM((3, 8, CH), F32),
             pltpu.VMEM((3, 128, CH), F32),
             dma((8,)), dma((8,)), dma((2,)), dma((2,)), dma((2,)), dma((2,)), dma((8,)), dma((8,)), dma((3,)),
-            dma((3, 7)), dma((3, 7)), dma((3, 15)), dma((3, 15)),
-            dma((3, 15)), dma((3, 15)), dma((3, 7)), dma((3, 7)),
+            dma((3,)), dma((3,)), dma((3,)), dma((3,)), dma((3,)), dma((3,)), dma((3,)), dma((3,)),
         ],
         compiler_params=pltpu.CompilerParams(
             collective_id=0, has_side_effects=True, vmem_limit_bytes=56 * 1024 * 1024

time: 91.2 us -> 88.5 us (0.970)
  Pallas kernels: 90.2 us -> 87.5 us
    pallas_call x1, Pallas kernels: 87.3 us -> 84.6 us  [run_kernel(): pl.pallas_call(kernel, out_shape=(jax.ShapeDtypeStruct((9 * CH, CH), F32)...]
where the time goes in v4:
time: 88.5 us; the launch traced here: 88.3 us
  Pallas kernels  87.5 us (99%)
    pallas_call x1, Pallas kernels, run_kernel(): pl.pallas_call(kernel, out_shape=(jax.ShapeDtypeStruct((9 * CH, CH), F32)...  84.6 us
    pallas_call x1, Pallas kernels, hand_over(): pl.pallas_call(hand_over_kernel, out_shape=(jax.ShapeDtypeStruct((1, 1),...  2.88 us

profile of v4, /device:TPU:1, one launch (start us, length us, event | category | flops | bytes accessed | tf_op | source)
XLA Modules:
  0.0 88.3 jit_solution(6295190324305211557)
XLA Ops:
  0.6 84.6 %shard_map.183 = (f32[1152,128]{1,0:T(8,128)}, f32[1152,128]{1,0:T(8,128)}, f32[104,128]{1,0:T(8,128)}) custom-call(bf16[16,128,128]{2,1,0:T(8,128)(2,1)} %feat.1, bf16[3,3,128,128]{3,2,1,0:T(8,128)(2,1)} %w1.1, f32[1,128]{1,0:T(1,128)} %bitcast.23, bf16[3,3,128,128]{3,2,1,0:T(8,128)(2,1)} %w2.1, f32[1,128]{1,0:T(1,128)} %bitcast.24, ...), custom_call_target="tpu_custom_call" | custom-call | tf_op jit(solution)/shard_map/pallas_call | solution.py:672
  85.3 2.9 %shard_map.184 = (f32[1,1]{1,0:T(1,128)}, f32[1152,128]{1,0:T(8,128)}, f32[1152,128]{1,0:T(8,128)}, f32[3,3,3,128]{3,2,1,0:T(4,128)}) custom-call(f32[1152,128]{1,0:T(8,128)} %get-tuple-element.11.one, f32[1152,128]{1,0:T(8,128)} %get-tuple-element.12.two, f32[104,128]{1,0:T(8,128)} %get-tuple-element.13.rest), custom_call_target="tpu_custom_call" | custom-call | tf_op jit(solution)/shard_map/pallas_call | solution.py:751

commit v5 on v4

--- a/solution.py
+++ b/solution.py
@@ -213,7 +213,7 @@
 
 
 def vgg_first(zs, fs, v1, v1b, n):
-    @pl.loop(0, TROWS // n, unroll=4)
+    @pl.loop(0, TROWS // n, unroll=8)
     def _(k):
         r0 = k * n
         rhs = jnp.concatenate(
@@ -257,7 +257,7 @@
         peer = device([(xyz[i] + off[i]) % 4 for i in range(3)], (core + off[3]) % 2)
         pl.semaphore_signal(barrier, inc=1, device_id=peer, device_id_type=MESH)
 
-    @pl.loop(0, 8, unroll=4)
+    @pl.loop(0, 8, unroll=8)
     def _(k):
         at = span(k * 1024, 1024, 128)
         index = tap_i[:, at]
@@ -358,7 +358,7 @@
             [tgt, jnp.zeros((5, 128), F32)], axis=0
         )
 
-    @pl.loop(0, 8, unroll=4)
+    @pl.loop(0, 8, unroll=8)
     def _(k):
         store_scaled(zs, unit_t[0:8, span(k * 1024, 1024, 128)], k * 8, 8)
 
@@ -402,7 +402,7 @@
 
     clear(a1, 2)
 
-    @pl.loop(0, 6, unroll=3)
+    @pl.loop(0, 6, unroll=6)
     def _(k):
         r = k * 3
         f = f_ref[pl.ds(r + 2, 3)].reshape(3 * WIDE, CH).astype(F32)
@@ -434,7 +434,7 @@
         copy.start()
         colours.append(copy)
 
-    @pl.loop(0, TROWS // 4, unroll=4)
+    @pl.loop(0, TROWS // 4, unroll=8)
     def _(k):
         f = jnp.maximum(dot(v2c[...], nine_taps(fs, k * 4, 4)) + v2b_col, 0.0)
         unit_t[:, span(k * 512, 512, 128)] = f * inv_norm(f)
@@ -456,7 +456,7 @@
     table_lo = (table - table_hi.astype(F32)).astype(BF)
     table = jnp.concatenate([table_hi, table_lo], axis=0)
 
-    @pl.loop(0, 8, unroll=4)
+    @pl.loop(0, 8, unroll=8)
     def _(k):
         at = span(k * 1024, 1024, 128)
         got = dot(table, hot[:, at])
@@ -476,7 +476,7 @@
     vgg_first(zs, fs, v1, v1b_col, 4)
     loss_acc[...] = jnp.zeros_like(loss_acc)
 
-    @pl.loop(0, TROWS // 4, unroll=4)
+    @pl.loop(0, TROWS // 4, unroll=8)
     def _(k):
         f = jnp.maximum(dot(v2c[...], nine_taps(fs, k * 4, 4)) + v2b_col, 0.0)
         inv = inv_norm(f)
@@ -503,7 +503,7 @@
         axis=0,
     ).astype(BF)
 
-    @pl.loop(0, TROWS // 4, unroll=4)
+    @pl.loop(0, TROWS // 4, unroll=8)
     def _(k):
         g = dot(v2t[...], nine_taps(gs, k * 4, 4)).astype(BF)
         at = span((k * 4 + 1) * 128, 512, 128)
@@ -534,7 +534,7 @@
         lo = (spread - hi.astype(F32)).astype(BF)
         return acc + dot(jnp.concatenate([hi, lo], axis=0), hot[:, at], 1, 1)
 
-    acc = lax.fori_loop(0, 8, table_adjoint, jnp.zeros((96, 384), F32), unroll=4)
+    acc = lax.fori_loop(0, 8, table_adjoint, jnp.zeros((96, 384), F32), unroll=8)
     acc = acc[0:48] + acc[48:96]
     adjoint = acc[0:24] + pltpu.roll(acc[24:48], 1, 1)
     for k in range(3):

time: 88.5 us -> 87.3 us (0.986)
  Pallas kernels: 87.5 us -> 86.3 us
    pallas_call x1, Pallas kernels: 84.6 us -> 83.4 us  [run_kernel(): pl.pallas_call(kernel, out_shape=(jax.ShapeDtypeStruct((9 * CH, CH), F32)...]
where the time goes in v5:
time: 87.3 us; the launch traced here: 87.1 us
  Pallas kernels  86.3 us (99%)
    pallas_call x1, Pallas kernels, run_kernel(): pl.pallas_call(kernel, out_shape=(jax.ShapeDtypeStruct((9 * CH, CH), F32)...  83.4 us
    pallas_call x1, Pallas kernels, hand_over(): pl.pallas_call(hand_over_kernel, out_shape=(jax.ShapeDtypeStruct((1, 1),...  2.88 us

profile of v5, /device:TPU:1, one launch (start us, length us, event | category | flops | bytes accessed | tf_op | source)
XLA Modules:
  0.0 87.1 jit_solution(11156026800281850016)
XLA Ops:
  0.6 83.4 %shard_map.183 = (f32[1152,128]{1,0:T(8,128)}, f32[1152,128]{1,0:T(8,128)}, f32[104,128]{1,0:T(8,128)}) custom-call(bf16[16,128,128]{2,1,0:T(8,128)(2,1)} %feat.1, bf16[3,3,128,128]{3,2,1,0:T(8,128)(2,1)} %w1.1, f32[1,128]{1,0:T(1,128)} %bitcast.23, bf16[3,3,128,128]{3,2,1,0:T(8,128)(2,1)} %w2.1, f32[1,128]{1,0:T(1,128)} %bitcast.24, ...), custom_call_target="tpu_custom_call" | custom-call | tf_op jit(solution)/shard_map/pallas_call | solution.py:672
  84.0 2.9 %shard_map.184 = (f32[1,1]{1,0:T(1,128)}, f32[1152,128]{1,0:T(8,128)}, f32[1152,128]{1,0:T(8,128)}, f32[3,3,3,128]{3,2,1,0:T(4,128)}) custom-call(f32[1152,128]{1,0:T(8,128)} %get-tuple-element.11.one, f32[1152,128]{1,0:T(8,128)} %get-tuple-element.12.two, f32[104,128]{1,0:T(8,128)} %get-tuple-element.13.rest), custom_call_target="tpu_custom_call" | custom-call | tf_op jit(solution)/shard_map/pallas_call | solution.py:751
